TPU v7x, 32 devices: a whole 2x2x4 slice. The times are simulated.
32 devices in a mesh: ctx: 8 (over z, x), head: 4 (over y, core).
Axes of the slice: x: 2, y: 2, z: 4, core: 2. Of those that a mesh axis runs over, the one named last changes fastest.
Arguments:
- queries: bfloat16 [512, 16, 128], P('ctx', 'head'), may hold values from -9 to 9
- cache_keys: bfloat16 [16384, 128], P('ctx'), may hold values from -15 to 15
- cache_values: bfloat16 [16384, 128], P('ctx'), may hold values from -6 to 6
- page_table: int32 [8, 4], P('ctx'), may hold values from 0 to 3, each once within a row
- page_count: int32 [8], P('ctx'), may hold values from 1 to 4, as said below
- new_kv: bfloat16 [512, 2, 128], P(('ctx', 'head')), may hold values from -15 to 15
- new_owner: int32 [512], replicated, may hold values from 0 to 7, as said below
- new_offset: int32 [512], replicated, may hold values from 0 to 127
Outputs:
- attended: bfloat16 [512, 16, 128], P('ctx', 'head')
- appended: bfloat16 [1024, 2, 128], P('ctx')
Inputs may be any that keep to these rules, and one draw needn't show every extreme that they name: `page_count`: some store has all 4 pages live. `page_table`: each row names every page once. `new_owner`: no two new tokens share a pair of owner and offset; some store's 128 rows are all taken.
All inputs are finite; a program needn't handle non-finite values.
Results may differ from a plain program's by a relative error of at most 0.0028.
Values may be sent and summed in bfloat16 or wider, within the bound.
A program may use at most 64 MiB of HBM per device.

v0:
```python
import math

import jax
import jax.numpy as jnp
from jax import lax
from jax.sharding import PartitionSpec as P


def passed_along(value, axis, steps):
    count = lax.axis_size(axis)
    pairs = [(source, (source + steps) % count) for source in range(count)]
    return lax.ppermute(value, axis, pairs)


def cache_part(query_rows, cache_keys, cache_values, table_row, live_count, scaling):
    page_rows = cache_keys.shape[0] // table_row.shape[0]
    count_rows = query_rows.shape[0]

    def take_page(number, carry):
        maxima, totals, summed = carry
        page_index = lax.dynamic_index_in_dim(table_row, number, 0, keepdims=False)
        key_block = lax.dynamic_slice_in_dim(cache_keys, page_index * page_rows, page_rows, 0)
        value_block = lax.dynamic_slice_in_dim(cache_values, page_index * page_rows, page_rows, 0)
        scores = (
            lax.dot_general(
                query_rows, key_block, (((1,), (1,)), ((), ())), preferred_element_type=jnp.float32
            )
            * scaling
        )
        updated = jnp.maximum(maxima, jnp.max(scores, axis=1))
        factor = jnp.exp(maxima - updated)
        weights = jnp.exp(scores - updated[:, None])
        totals = totals * factor + jnp.sum(weights, axis=1)
        summed = summed * factor[:, None] + jnp.dot(
            weights.astype(jnp.bfloat16), value_block, preferred_element_type=jnp.float32
        )
        return (updated, totals, summed)

    initial = (
        jnp.full((count_rows,), -1e30, jnp.float32),
        jnp.zeros((count_rows,), jnp.float32),
        jnp.zeros((count_rows, query_rows.shape[1]), jnp.float32),
    )
    return lax.fori_loop(0, live_count, take_page, initial)


def join_partials(first, second):
    combined = jnp.maximum(first[0], second[0])
    factor_one = jnp.exp(first[0] - combined)
    factor_two = jnp.exp(second[0] - combined)
    totals = first[1] * factor_one + second[1] * factor_two
    summed = first[2] * factor_one[..., None] + second[2] * factor_two[..., None]
    return (combined, totals, summed)


def shards(
    queries, cache_keys, cache_values, page_table, page_count, new_kv, new_owner, new_offset
):
    tok_dev, head_dev, head_size = queries.shape
    stores = lax.axis_size("ctx")
    own_store = lax.axis_index("ctx")
    scaling = 1.0 / math.sqrt(head_size)
    table_row = page_table[0]
    live_count = page_count[0]

    def local_part(query_rows):
        return cache_part(query_rows, cache_keys, cache_values, table_row, live_count, scaling)

    def travel_step(number, carry):
        visiting, maxima, totals, summed = carry
        found = local_part(visiting.reshape(tok_dev * head_dev, head_size))
        found = (
            found[0].reshape(tok_dev, head_dev),
            found[1].reshape(tok_dev, head_dev),
            found[2].reshape(tok_dev, head_dev, head_size),
        )
        maxima, totals, summed = join_partials((maxima, totals, summed), found)
        visiting = passed_along(visiting, "ctx", 1)
        summed, maxima, totals = passed_along((summed, maxima, totals), "ctx", 1)
        return (visiting, maxima, totals, summed)

    initial = (
        queries,
        jnp.full((tok_dev, head_dev), -1e30, jnp.float32),
        jnp.zeros((tok_dev, head_dev), jnp.float32),
        jnp.zeros((tok_dev, head_dev, head_size), jnp.float32),
    )
    visited, cache_max, cache_total, cache_sum = lax.fori_loop(0, stores, travel_step, initial)
    new_rows = lax.all_gather(new_kv, ("ctx", "head"), axis=0, tiled=True)
    query_rows = queries.reshape(tok_dev * head_dev, head_size)
    scores = (
        lax.dot_general(
            query_rows, new_rows[:, 0], (((1,), (1,)), ((), ())), preferred_element_type=jnp.float32
        )
        * scaling
    )
    positions = own_store * tok_dev + jnp.arange(tok_dev * head_dev, dtype=jnp.int32) // head_dev
    visible = jnp.arange(new_rows.shape[0], dtype=jnp.int32)[None, :] <= positions[:, None]
    scores = jnp.where(visible, scores, jnp.float32(-1e30))
    self_max = jnp.max(scores, axis=1)
    weights = jnp.exp(scores - self_max[:, None])
    self_total = jnp.sum(weights, axis=1)
    self_sum = jnp.dot(
        weights.astype(jnp.bfloat16), new_rows[:, 1], preferred_element_type=jnp.float32
    )
    self_part = (
        self_max.reshape(tok_dev, head_dev),
        self_total.reshape(tok_dev, head_dev),
        self_sum.reshape(tok_dev, head_dev, head_size),
    )
    maxima, totals, summed = join_partials((cache_max, cache_total, cache_sum), self_part)
    attended = (summed / totals[..., None]).astype(jnp.bfloat16)
    append_rows = 2 * tok_dev
    target = jnp.where(new_owner == own_store, new_offset, append_rows)
    appended = (
        jnp.zeros((append_rows, 2, head_size), jnp.bfloat16).at[target].set(new_rows, mode="drop")
    )
    return (attended, appended)


def solution(mesh):
    in_specs = (
        P("ctx", "head", None),
        P("ctx", None),
        P("ctx", None),
        P("ctx", None),
        P("ctx"),
        P(("ctx", "head"), None, None),
        P(),
        P(),
    )
    out_specs = (P("ctx", "head", None), P("ctx", None, None))
    return jax.shard_map(shards, mesh=mesh, in_specs=in_specs, out_specs=out_specs, check_vma=False)
```

profile of v0, /device:TPU:0, one launch (start us, length us, event | category | flops | bytes accessed | tf_op | source)
XLA Modules:
  0.0 277.4 jit_solution(14454744427687482692)
XLA Ops:
  2.9 216.8 %while.31 = (s32[]{:T(128)}, bf16[64,4,128]{2,1,0:T(4,128)(2,1)S(1)}, f32[64,4]{1,0:T(8,128)S(1)}, f32[64,4]{1,0:T(8,128)S(1)}, f32[64,4,128]{2,1,0:T(4,128)S(1)...) while((s32[]{:T(128)}, ...), condition=%wide.region_5.6_spmd, body=%wide.region_0.5_spmd.sunk | while | flops 68061192 | bytes 3646146 | solution.py:88
  2.9 9.5 %while.32 = (s32[]{:T(128)}, f32[256]{0:T(256)S(1)}, f32[256]{0:T(256)S(1)}, f32[256,128]{1,0:T(8,128)S(1)}, s32[]{:T(128)}, /*index=5*/s32[4]{0:T(128)S(1)}, bf...) while((s32[]{:T(128)}, f32[256]{0:T(256)S(1)}, ...), condition=%wide.region_4.4_spmd, body=%wide.region_1.3_spmd.sunk | while | flops 67961352 | bytes 2179313 | solution.py:44
  15.9 10.4 %collective-permute-start = (bf16[64,4,128]{2,1,0:T(4,128)(2,1)S(1)}, bf16[64,4,128]{2,1,0:T(4,128)(2,1)S(1)}, u32[]{:S(2)}, u32[]{:S(2)}) collective-permute-start(bf16[64,4,128]{2,1,0:T(4,128)(2,1)S(1)} %bitcast.28), channel_id=1, source_target_pairs={{0,4},{4,8},{8,12},{12,16},{16,20},{20,24},{24,28},{28,0},{1,5},{5... | collective-permute-start | bytes 196616 | tf_op jit(solution)/shard_map/while/body/eval_jaxpr/ppermute | solution.py:12
  26.5 6.5 %collective-permute-done.1 = f32[64,4]{1,0:T(8,128)S(1)} collective-permute-done((f32[64,4]{1,0:T(8,128)S(1)}, f32[64,4]{1,0:T(8,128)S(1)}, u32[]{:S(2)}, u32[]{:S(2)}) %collective-permute-start.1) | collective-permute-done | bytes 1056 | tf_op jit(solution)/shard_map/while/body/eval_jaxpr/ppermute | solution.py:12
  33.4 9.5 %while.32 = (s32[]{:T(128)}, f32[256]{0:T(256)S(1)}, f32[256]{0:T(256)S(1)}, f32[256,128]{1,0:T(8,128)S(1)}, s32[]{:T(128)}, /*index=5*/s32[4]{0:T(128)S(1)}, bf...) while((s32[]{:T(128)}, f32[256]{0:T(256)S(1)}, ...), condition=%wide.region_4.4_spmd, body=%wide.region_1.3_spmd.sunk | while | flops 67961352 | bytes 2179313 | solution.py:44
  43.5 10.8 %collective-permute-start = (bf16[64,4,128]{2,1,0:T(4,128)(2,1)S(1)}, bf16[64,4,128]{2,1,0:T(4,128)(2,1)S(1)}, u32[]{:S(2)}, u32[]{:S(2)}) collective-permute-start(bf16[64,4,128]{2,1,0:T(4,128)(2,1)S(1)} %bitcast.28), channel_id=1, source_target_pairs={{0,4},{4,8},{8,12},{12,16},{16,20},{20,24},{24,28},{28,0},{1,5},{5... | collective-permute-start | bytes 196616 | tf_op jit(solution)/shard_map/while/body/eval_jaxpr/ppermute | solution.py:12
  54.4 6.5 %collective-permute-done.1 = f32[64,4]{1,0:T(8,128)S(1)} collective-permute-done((f32[64,4]{1,0:T(8,128)S(1)}, f32[64,4]{1,0:T(8,128)S(1)}, u32[]{:S(2)}, u32[]{:S(2)}) %collective-permute-start.1) | collective-permute-done | bytes 1056 | tf_op jit(solution)/shard_map/while/body/eval_jaxpr/ppermute | solution.py:12
  61.3 9.5 %while.32 = (s32[]{:T(128)}, f32[256]{0:T(256)S(1)}, f32[256]{0:T(256)S(1)}, f32[256,128]{1,0:T(8,128)S(1)}, s32[]{:T(128)}, /*index=5*/s32[4]{0:T(128)S(1)}, bf...) while((s32[]{:T(128)}, f32[256]{0:T(256)S(1)}, ...), condition=%wide.region_4.4_spmd, body=%wide.region_1.3_spmd.sunk | while | flops 67961352 | bytes 2179313 | solution.py:44
  71.4 10.0 %collective-permute-start = (bf16[64,4,128]{2,1,0:T(4,128)(2,1)S(1)}, bf16[64,4,128]{2,1,0:T(4,128)(2,1)S(1)}, u32[]{:S(2)}, u32[]{:S(2)}) collective-permute-start(bf16[64,4,128]{2,1,0:T(4,128)(2,1)S(1)} %bitcast.28), channel_id=1, source_target_pairs={{0,4},{4,8},{8,12},{12,16},{16,20},{20,24},{24,28},{28,0},{1,5},{5... | collective-permute-start | bytes 196616 | tf_op jit(solution)/shard_map/while/body/eval_jaxpr/ppermute | solution.py:12
  81.5 6.5 %collective-permute-done.1 = f32[64,4]{1,0:T(8,128)S(1)} collective-permute-done((f32[64,4]{1,0:T(8,128)S(1)}, f32[64,4]{1,0:T(8,128)S(1)}, u32[]{:S(2)}, u32[]{:S(2)}) %collective-permute-start.1) | collective-permute-done | bytes 1056 | tf_op jit(solution)/shard_map/while/body/eval_jaxpr/ppermute | solution.py:12
  88.4 9.5 %while.32 = (s32[]{:T(128)}, f32[256]{0:T(256)S(1)}, f32[256]{0:T(256)S(1)}, f32[256,128]{1,0:T(8,128)S(1)}, s32[]{:T(128)}, /*index=5*/s32[4]{0:T(128)S(1)}, bf...) while((s32[]{:T(128)}, f32[256]{0:T(256)S(1)}, ...), condition=%wide.region_4.4_spmd, body=%wide.region_1.3_spmd.sunk | while | flops 67961352 | bytes 2179313 | solution.py:44
  98.5 9.2 %collective-permute-start = (bf16[64,4,128]{2,1,0:T(4,128)(2,1)S(1)}, bf16[64,4,128]{2,1,0:T(4,128)(2,1)S(1)}, u32[]{:S(2)}, u32[]{:S(2)}) collective-permute-start(bf16[64,4,128]{2,1,0:T(4,128)(2,1)S(1)} %bitcast.28), channel_id=1, source_target_pairs={{0,4},{4,8},{8,12},{12,16},{16,20},{20,24},{24,28},{28,0},{1,5},{5... | collective-permute-start | bytes 196616 | tf_op jit(solution)/shard_map/while/body/eval_jaxpr/ppermute | solution.py:12
  114.7 9.5 %while.32 = (s32[]{:T(128)}, f32[256]{0:T(256)S(1)}, f32[256]{0:T(256)S(1)}, f32[256,128]{1,0:T(8,128)S(1)}, s32[]{:T(128)}, /*index=5*/s32[4]{0:T(128)S(1)}, bf...) while((s32[]{:T(128)}, f32[256]{0:T(256)S(1)}, ...), condition=%wide.region_4.4_spmd, body=%wide.region_1.3_spmd.sunk | while | flops 67961352 | bytes 2179313 | solution.py:44
  124.8 9.2 %collective-permute-start = (bf16[64,4,128]{2,1,0:T(4,128)(2,1)S(1)}, bf16[64,4,128]{2,1,0:T(4,128)(2,1)S(1)}, u32[]{:S(2)}, u32[]{:S(2)}) collective-permute-start(bf16[64,4,128]{2,1,0:T(4,128)(2,1)S(1)} %bitcast.28), channel_id=1, source_target_pairs={{0,4},{4,8},{8,12},{12,16},{16,20},{20,24},{24,28},{28,0},{1,5},{5... | collective-permute-start | bytes 196616 | tf_op jit(solution)/shard_map/while/body/eval_jaxpr/ppermute | solution.py:12
  134.1 6.5 %collective-permute-done.1 = f32[64,4]{1,0:T(8,128)S(1)} collective-permute-done((f32[64,4]{1,0:T(8,128)S(1)}, f32[64,4]{1,0:T(8,128)S(1)}, u32[]{:S(2)}, u32[]{:S(2)}) %collective-permute-start.1) | collective-permute-done | bytes 1056 | tf_op jit(solution)/shard_map/while/body/eval_jaxpr/ppermute | solution.py:12
  141.0 9.5 %while.32 = (s32[]{:T(128)}, f32[256]{0:T(256)S(1)}, f32[256]{0:T(256)S(1)}, f32[256,128]{1,0:T(8,128)S(1)}, s32[]{:T(128)}, /*index=5*/s32[4]{0:T(128)S(1)}, bf...) while((s32[]{:T(128)}, f32[256]{0:T(256)S(1)}, ...), condition=%wide.region_4.4_spmd, body=%wide.region_1.3_spmd.sunk | while | flops 67961352 | bytes 2179313 | solution.py:44
  151.0 9.2 %collective-permute-start = (bf16[64,4,128]{2,1,0:T(4,128)(2,1)S(1)}, bf16[64,4,128]{2,1,0:T(4,128)(2,1)S(1)}, u32[]{:S(2)}, u32[]{:S(2)}) collective-permute-start(bf16[64,4,128]{2,1,0:T(4,128)(2,1)S(1)} %bitcast.28), channel_id=1, source_target_pairs={{0,4},{4,8},{8,12},{12,16},{16,20},{20,24},{24,28},{28,0},{1,5},{5... | collective-permute-start | bytes 196616 | tf_op jit(solution)/shard_map/while/body/eval_jaxpr/ppermute | solution.py:12
  160.3 6.5 %collective-permute-done.1 = f32[64,4]{1,0:T(8,128)S(1)} collective-permute-done((f32[64,4]{1,0:T(8,128)S(1)}, f32[64,4]{1,0:T(8,128)S(1)}, u32[]{:S(2)}, u32[]{:S(2)}) %collective-permute-start.1) | collective-permute-done | bytes 1056 | tf_op jit(solution)/shard_map/while/body/eval_jaxpr/ppermute | solution.py:12
  167.2 9.5 %while.32 = (s32[]{:T(128)}, f32[256]{0:T(256)S(1)}, f32[256]{0:T(256)S(1)}, f32[256,128]{1,0:T(8,128)S(1)}, s32[]{:T(128)}, /*index=5*/s32[4]{0:T(128)S(1)}, bf...) while((s32[]{:T(128)}, f32[256]{0:T(256)S(1)}, ...), condition=%wide.region_4.4_spmd, body=%wide.region_1.3_spmd.sunk | while | flops 67961352 | bytes 2179313 | solution.py:44
  177.3 9.2 %collective-permute-start = (bf16[64,4,128]{2,1,0:T(4,128)(2,1)S(1)}, bf16[64,4,128]{2,1,0:T(4,128)(2,1)S(1)}, u32[]{:S(2)}, u32[]{:S(2)}) collective-permute-start(bf16[64,4,128]{2,1,0:T(4,128)(2,1)S(1)} %bitcast.28), channel_id=1, source_target_pairs={{0,4},{4,8},{8,12},{12,16},{16,20},{20,24},{24,28},{28,0},{1,5},{5... | collective-permute-start | bytes 196616 | tf_op jit(solution)/shard_map/while/body/eval_jaxpr/ppermute | solution.py:12
  193.5 9.5 %while.32 = (s32[]{:T(128)}, f32[256]{0:T(256)S(1)}, f32[256]{0:T(256)S(1)}, f32[256,128]{1,0:T(8,128)S(1)}, s32[]{:T(128)}, /*index=5*/s32[4]{0:T(128)S(1)}, bf...) while((s32[]{:T(128)}, f32[256]{0:T(256)S(1)}, ...), condition=%wide.region_4.4_spmd, body=%wide.region_1.3_spmd.sunk | while | flops 67961352 | bytes 2179313 | solution.py:44
  203.6 9.2 %collective-permute-start = (bf16[64,4,128]{2,1,0:T(4,128)(2,1)S(1)}, bf16[64,4,128]{2,1,0:T(4,128)(2,1)S(1)}, u32[]{:S(2)}, u32[]{:S(2)}) collective-permute-start(bf16[64,4,128]{2,1,0:T(4,128)(2,1)S(1)} %bitcast.28), channel_id=1, source_target_pairs={{0,4},{4,8},{8,12},{12,16},{16,20},{20,24},{24,28},{28,0},{1,5},{5... | collective-permute-start | bytes 196616 | tf_op jit(solution)/shard_map/while/body/eval_jaxpr/ppermute | solution.py:12
  219.7 39.6 %all_gather.3 = bf16[512,2,128]{2,0,1:T(8,128)(2,1)S(1)} all-gather(bf16[16,2,128]{2,0,1:T(8,128)(2,1)S(1)} %copy.17), channel_id=1, replica_groups=mesh['ctx'=8,'head'=4] {'ctx','head'}, dimensions={0}, use_global_device_ids=true | all-gather | bytes 270336 | tf_op jit(solution)/shard_map/all_gather | solution.py:89
  259.7 15.4 %scatter_fusion = bf16[128,2,128]{2,1,0:T(2,128)(2,1)S(1)} fusion(bf16[128,2,128]{2,1,0:T(2,128)(2,1)S(1)} %broadcast_in_dim.37, s32[512]{0:T(512)S(1)} %compare_select_fusion, bf16[512,2,128]{2,1,0:T(2,128)(2,1)S(1)} %copy.23), kind=kCustom, calls=%fused_computation | custom fusion | bytes 788480 | tf_op jit(solution)/shard_map/scatter | solution.py:116
  (259 shorter events, 85.3 us)
Async XLA Ops:
  12.9 20.4 %collective-permute-start.3 = (f32[64,4,128]{2,1,0:T(4,128)S(1)}, f32[64,4,128]{2,1,0:T(4,128)S(1)}, u32[]{:S(2)}, u32[]{:S(2)}) collective-permute-start(f32[64,4,128]{2,1,0:T(4,128)S(1)} %multiply_add_fusion.8), channel_id=1, source_target_pairs={{0,4},{4,8},{8,12},{12,16},{16,20},{20,24},{24,28},{28,0},{1,5},{5... | collective-permute-start | bytes 393224 | tf_op jit(solution)/shard_map/while/body/eval_jaxpr/ppermute | solution.py:12
  15.9 17.4 %collective-permute-start = (bf16[64,4,128]{2,1,0:T(4,128)(2,1)S(1)}, bf16[64,4,128]{2,1,0:T(4,128)(2,1)S(1)}, u32[]{:S(2)}, u32[]{:S(2)}) collective-permute-start(bf16[64,4,128]{2,1,0:T(4,128)(2,1)S(1)} %bitcast.28), channel_id=1, source_target_pairs={{0,4},{4,8},{8,12},{12,16},{16,20},{20,24},{24,28},{28,0},{1,5},{5... | collective-permute-start | bytes 196616 | tf_op jit(solution)/shard_map/while/body/eval_jaxpr/ppermute | solution.py:12
  26.4 6.9 %collective-permute-start.2 = (f32[64,4]{1,0:T(8,128)S(1)}, f32[64,4]{1,0:T(8,128)S(1)}, u32[]{:S(2)}, u32[]{:S(2)}) collective-permute-start(f32[64,4]{1,0:T(8,128)S(1)} %get-tuple-element.294), channel_id=1, source_target_pairs={{0,4},{4,8},{8,12},{12,16},{16,20},{20,24},{24,28},{28,0},{1,5},{5... | collective-permute-start | bytes 3080 | tf_op jit(solution)/shard_map/while/body/eval_jaxpr/ppermute | solution.py:12
  43.4 17.9 %collective-permute-start.3 = (f32[64,4,128]{2,1,0:T(4,128)S(1)}, f32[64,4,128]{2,1,0:T(4,128)S(1)}, u32[]{:S(2)}, u32[]{:S(2)}) collective-permute-start(f32[64,4,128]{2,1,0:T(4,128)S(1)} %multiply_add_fusion.8), channel_id=1, source_target_pairs={{0,4},{4,8},{8,12},{12,16},{16,20},{20,24},{24,28},{28,0},{1,5},{5... | collective-permute-start | bytes 393224 | tf_op jit(solution)/shard_map/while/body/eval_jaxpr/ppermute | solution.py:12
  43.5 17.8 %collective-permute-start = (bf16[64,4,128]{2,1,0:T(4,128)(2,1)S(1)}, bf16[64,4,128]{2,1,0:T(4,128)(2,1)S(1)}, u32[]{:S(2)}, u32[]{:S(2)}) collective-permute-start(bf16[64,4,128]{2,1,0:T(4,128)(2,1)S(1)} %bitcast.28), channel_id=1, source_target_pairs={{0,4},{4,8},{8,12},{12,16},{16,20},{20,24},{24,28},{28,0},{1,5},{5... | collective-permute-start | bytes 196616 | tf_op jit(solution)/shard_map/while/body/eval_jaxpr/ppermute | solution.py:12
  54.4 6.9 %collective-permute-start.2 = (f32[64,4]{1,0:T(8,128)S(1)}, f32[64,4]{1,0:T(8,128)S(1)}, u32[]{:S(2)}, u32[]{:S(2)}) collective-permute-start(f32[64,4]{1,0:T(8,128)S(1)} %get-tuple-element.294), channel_id=1, source_target_pairs={{0,4},{4,8},{8,12},{12,16},{16,20},{20,24},{24,28},{28,0},{1,5},{5... | collective-permute-start | bytes 3080 | tf_op jit(solution)/shard_map/while/body/eval_jaxpr/ppermute | solution.py:12
  71.3 17.0 %collective-permute-start.3 = (f32[64,4,128]{2,1,0:T(4,128)S(1)}, f32[64,4,128]{2,1,0:T(4,128)S(1)}, u32[]{:S(2)}, u32[]{:S(2)}) collective-permute-start(f32[64,4,128]{2,1,0:T(4,128)S(1)} %multiply_add_fusion.8), channel_id=1, source_target_pairs={{0,4},{4,8},{8,12},{12,16},{16,20},{20,24},{24,28},{28,0},{1,5},{5... | collective-permute-start | bytes 393224 | tf_op jit(solution)/shard_map/while/body/eval_jaxpr/ppermute | solution.py:12
  71.4 16.9 %collective-permute-start = (bf16[64,4,128]{2,1,0:T(4,128)(2,1)S(1)}, bf16[64,4,128]{2,1,0:T(4,128)(2,1)S(1)}, u32[]{:S(2)}, u32[]{:S(2)}) collective-permute-start(bf16[64,4,128]{2,1,0:T(4,128)(2,1)S(1)} %bitcast.28), channel_id=1, source_target_pairs={{0,4},{4,8},{8,12},{12,16},{16,20},{20,24},{24,28},{28,0},{1,5},{5... | collective-permute-start | bytes 196616 | tf_op jit(solution)/shard_map/while/body/eval_jaxpr/ppermute | solution.py:12
  81.4 6.9 %collective-permute-start.2 = (f32[64,4]{1,0:T(8,128)S(1)}, f32[64,4]{1,0:T(8,128)S(1)}, u32[]{:S(2)}, u32[]{:S(2)}) collective-permute-start(f32[64,4]{1,0:T(8,128)S(1)} %get-tuple-element.294), channel_id=1, source_target_pairs={{0,4},{4,8},{8,12},{12,16},{16,20},{20,24},{24,28},{28,0},{1,5},{5... | collective-permute-start | bytes 3080 | tf_op jit(solution)/shard_map/while/body/eval_jaxpr/ppermute | solution.py:12
  98.4 16.2 %collective-permute-start.3 = (f32[64,4,128]{2,1,0:T(4,128)S(1)}, f32[64,4,128]{2,1,0:T(4,128)S(1)}, u32[]{:S(2)}, u32[]{:S(2)}) collective-permute-start(f32[64,4,128]{2,1,0:T(4,128)S(1)} %multiply_add_fusion.8), channel_id=1, source_target_pairs={{0,4},{4,8},{8,12},{12,16},{16,20},{20,24},{24,28},{28,0},{1,5},{5... | collective-permute-start | bytes 393224 | tf_op jit(solution)/shard_map/while/body/eval_jaxpr/ppermute | solution.py:12
  98.5 16.1 %collective-permute-start = (bf16[64,4,128]{2,1,0:T(4,128)(2,1)S(1)}, bf16[64,4,128]{2,1,0:T(4,128)(2,1)S(1)}, u32[]{:S(2)}, u32[]{:S(2)}) collective-permute-start(bf16[64,4,128]{2,1,0:T(4,128)(2,1)S(1)} %bitcast.28), channel_id=1, source_target_pairs={{0,4},{4,8},{8,12},{12,16},{16,20},{20,24},{24,28},{28,0},{1,5},{5... | collective-permute-start | bytes 196616 | tf_op jit(solution)/shard_map/while/body/eval_jaxpr/ppermute | solution.py:12
  107.7 6.9 %collective-permute-start.2 = (f32[64,4]{1,0:T(8,128)S(1)}, f32[64,4]{1,0:T(8,128)S(1)}, u32[]{:S(2)}, u32[]{:S(2)}) collective-permute-start(f32[64,4]{1,0:T(8,128)S(1)} %get-tuple-element.294), channel_id=1, source_target_pairs={{0,4},{4,8},{8,12},{12,16},{16,20},{20,24},{24,28},{28,0},{1,5},{5... | collective-permute-start | bytes 3080 | tf_op jit(solution)/shard_map/while/body/eval_jaxpr/ppermute | solution.py:12
  124.7 16.2 %collective-permute-start.3 = (f32[64,4,128]{2,1,0:T(4,128)S(1)}, f32[64,4,128]{2,1,0:T(4,128)S(1)}, u32[]{:S(2)}, u32[]{:S(2)}) collective-permute-start(f32[64,4,128]{2,1,0:T(4,128)S(1)} %multiply_add_fusion.8), channel_id=1, source_target_pairs={{0,4},{4,8},{8,12},{12,16},{16,20},{20,24},{24,28},{28,0},{1,5},{5... | collective-permute-start | bytes 393224 | tf_op jit(solution)/shard_map/while/body/eval_jaxpr/ppermute | solution.py:12
  124.8 16.1 %collective-permute-start = (bf16[64,4,128]{2,1,0:T(4,128)(2,1)S(1)}, bf16[64,4,128]{2,1,0:T(4,128)(2,1)S(1)}, u32[]{:S(2)}, u32[]{:S(2)}) collective-permute-start(bf16[64,4,128]{2,1,0:T(4,128)(2,1)S(1)} %bitcast.28), channel_id=1, source_target_pairs={{0,4},{4,8},{8,12},{12,16},{16,20},{20,24},{24,28},{28,0},{1,5},{5... | collective-permute-start | bytes 196616 | tf_op jit(solution)/shard_map/while/body/eval_jaxpr/ppermute | solution.py:12
  134.0 6.9 %collective-permute-start.2 = (f32[64,4]{1,0:T(8,128)S(1)}, f32[64,4]{1,0:T(8,128)S(1)}, u32[]{:S(2)}, u32[]{:S(2)}) collective-permute-start(f32[64,4]{1,0:T(8,128)S(1)} %get-tuple-element.294), channel_id=1, source_target_pairs={{0,4},{4,8},{8,12},{12,16},{16,20},{20,24},{24,28},{28,0},{1,5},{5... | collective-permute-start | bytes 3080 | tf_op jit(solution)/shard_map/while/body/eval_jaxpr/ppermute | solution.py:12
  151.0 16.2 %collective-permute-start.3 = (f32[64,4,128]{2,1,0:T(4,128)S(1)}, f32[64,4,128]{2,1,0:T(4,128)S(1)}, u32[]{:S(2)}, u32[]{:S(2)}) collective-permute-start(f32[64,4,128]{2,1,0:T(4,128)S(1)} %multiply_add_fusion.8), channel_id=1, source_target_pairs={{0,4},{4,8},{8,12},{12,16},{16,20},{20,24},{24,28},{28,0},{1,5},{5... | collective-permute-start | bytes 393224 | tf_op jit(solution)/shard_map/while/body/eval_jaxpr/ppermute | solution.py:12
  151.0 16.1 %collective-permute-start = (bf16[64,4,128]{2,1,0:T(4,128)(2,1)S(1)}, bf16[64,4,128]{2,1,0:T(4,128)(2,1)S(1)}, u32[]{:S(2)}, u32[]{:S(2)}) collective-permute-start(bf16[64,4,128]{2,1,0:T(4,128)(2,1)S(1)} %bitcast.28), channel_id=1, source_target_pairs={{0,4},{4,8},{8,12},{12,16},{16,20},{20,24},{24,28},{28,0},{1,5},{5... | collective-permute-start | bytes 196616 | tf_op jit(solution)/shard_map/while/body/eval_jaxpr/ppermute | solution.py:12
  160.3 6.9 %collective-permute-start.2 = (f32[64,4]{1,0:T(8,128)S(1)}, f32[64,4]{1,0:T(8,128)S(1)}, u32[]{:S(2)}, u32[]{:S(2)}) collective-permute-start(f32[64,4]{1,0:T(8,128)S(1)} %get-tuple-element.294), channel_id=1, source_target_pairs={{0,4},{4,8},{8,12},{12,16},{16,20},{20,24},{24,28},{28,0},{1,5},{5... | collective-permute-start | bytes 3080 | tf_op jit(solution)/shard_map/while/body/eval_jaxpr/ppermute | solution.py:12
  177.2 16.2 %collective-permute-start.3 = (f32[64,4,128]{2,1,0:T(4,128)S(1)}, f32[64,4,128]{2,1,0:T(4,128)S(1)}, u32[]{:S(2)}, u32[]{:S(2)}) collective-permute-start(f32[64,4,128]{2,1,0:T(4,128)S(1)} %multiply_add_fusion.8), channel_id=1, source_target_pairs={{0,4},{4,8},{8,12},{12,16},{16,20},{20,24},{24,28},{28,0},{1,5},{5... | collective-permute-start | bytes 393224 | tf_op jit(solution)/shard_map/while/body/eval_jaxpr/ppermute | solution.py:12
  177.3 16.1 %collective-permute-start = (bf16[64,4,128]{2,1,0:T(4,128)(2,1)S(1)}, bf16[64,4,128]{2,1,0:T(4,128)(2,1)S(1)}, u32[]{:S(2)}, u32[]{:S(2)}) collective-permute-start(bf16[64,4,128]{2,1,0:T(4,128)(2,1)S(1)} %bitcast.28), channel_id=1, source_target_pairs={{0,4},{4,8},{8,12},{12,16},{16,20},{20,24},{24,28},{28,0},{1,5},{5... | collective-permute-start | bytes 196616 | tf_op jit(solution)/shard_map/while/body/eval_jaxpr/ppermute | solution.py:12
  186.5 6.9 %collective-permute-start.2 = (f32[64,4]{1,0:T(8,128)S(1)}, f32[64,4]{1,0:T(8,128)S(1)}, u32[]{:S(2)}, u32[]{:S(2)}) collective-permute-start(f32[64,4]{1,0:T(8,128)S(1)} %get-tuple-element.294), channel_id=1, source_target_pairs={{0,4},{4,8},{8,12},{12,16},{16,20},{20,24},{24,28},{28,0},{1,5},{5... | collective-permute-start | bytes 3080 | tf_op jit(solution)/shard_map/while/body/eval_jaxpr/ppermute | solution.py:12
  203.5 16.2 %collective-permute-start.3 = (f32[64,4,128]{2,1,0:T(4,128)S(1)}, f32[64,4,128]{2,1,0:T(4,128)S(1)}, u32[]{:S(2)}, u32[]{:S(2)}) collective-permute-start(f32[64,4,128]{2,1,0:T(4,128)S(1)} %multiply_add_fusion.8), channel_id=1, source_target_pairs={{0,4},{4,8},{8,12},{12,16},{16,20},{20,24},{24,28},{28,0},{1,5},{5... | collective-permute-start | bytes 393224 | tf_op jit(solution)/shard_map/while/body/eval_jaxpr/ppermute | solution.py:12
  203.6 16.1 %collective-permute-start = (bf16[64,4,128]{2,1,0:T(4,128)(2,1)S(1)}, bf16[64,4,128]{2,1,0:T(4,128)(2,1)S(1)}, u32[]{:S(2)}, u32[]{:S(2)}) collective-permute-start(bf16[64,4,128]{2,1,0:T(4,128)(2,1)S(1)} %bitcast.28), channel_id=1, source_target_pairs={{0,4},{4,8},{8,12},{12,16},{16,20},{20,24},{24,28},{28,0},{1,5},{5... | collective-permute-start | bytes 196616 | tf_op jit(solution)/shard_map/while/body/eval_jaxpr/ppermute | solution.py:12
  212.8 6.9 %collective-permute-start.2 = (f32[64,4]{1,0:T(8,128)S(1)}, f32[64,4]{1,0:T(8,128)S(1)}, u32[]{:S(2)}, u32[]{:S(2)}) collective-permute-start(f32[64,4]{1,0:T(8,128)S(1)} %get-tuple-element.294), channel_id=1, source_target_pairs={{0,4},{4,8},{8,12},{12,16},{16,20},{20,24},{24,28},{28,0},{1,5},{5... | collective-permute-start | bytes 3080 | tf_op jit(solution)/shard_map/while/body/eval_jaxpr/ppermute | solution.py:12
  (14 other events, 71.7 us)
where the time goes:
time: 276 us; the launch traced here: 277 us
  starting transfers between devices  81.5 us (30%)
  waiting for transfers between devices  54.7 us (20%)
  blocking collectives  39.6 us (14%)
  matrix products  38.7 us (14%)
  local copies, waits for them, and re-layouts  30.9 us (11%)
  loops' own time  26.8 us (10%)
  other arithmetic  4.4 us (2%)
    ppermute x32, starting transfers between devices, passed_along(): return lax.ppermute(value, axis, pairs)  81.5 us
    ppermute x32, waiting for transfers between devices, passed_along(): return lax.ppermute(value, axis, pairs)  54.7 us
    all_gather x1, blocking collectives, shards(): new_rows = lax.all_gather(new_kv, ('ctx', 'head'), axis=0, tiled=True)  39.6 us
    another operation x8, loops' own time, cache_part(): return lax.fori_loop(0, live_count, take_page, initial)  26.2 us
    dot_general x16, matrix products, take_page(): jnp.dot(weights.astype(jnp.bfloat16), value_block, preferred_element_type...  19.4 us
    dot_general x16, matrix products, take_page(): lax.dot_general(query_rows, key_block, (((1,), (1,)), ((), ())), preferre...  18.7 us
    scatter x1, local copies, waits for them, and re-layouts, shards(): jnp.zeros((append_rows, 2, head_size), jnp.bfloat16).at[target]  15.4 us
    dynamic_slice x16, local copies, waits for them, and re-layouts, take_page(): page_index = lax.dynamic_index_in_dim(table_row, number, 0, keepdims=False)  9.53 us
  transfers between devices with their start and end apart: 32, of which 16 were waited for; matrix products, arithmetic and copies ran while one was open for 0% of the time, Pallas kernels for 0%

commit v1 on v0

v1 whole, which is shorter than its diff:
```python
import functools
import math

import jax
import jax.numpy as jnp
from jax import lax
from jax.experimental import pallas as pl
from jax.experimental.pallas import tpu as pltpu
from jax.sharding import PartitionSpec as P

MESH = pl.DeviceIdType.MESH
FAR = 1e30
STEPS = 32767.0
TINY = 1e-30
NT = (((1,), (1,)), ((), ()))


def attention_kernel(
    layers,
    heads_axis,
    head_dev,
    slots,
    table_ref,
    count_ref,
    queries_ref,
    keys_ref,
    values_ref,
    new_ref,
    owner_ref,
    offset_ref,
    attended_ref,
    appended_ref,
    k_ref,
    v_ref,
    qz_ref,
    qx_ref,
    own_o,
    own_l,
    sx_o,
    sx_l,
    rx_o,
    rx_l,
    sz_o,
    sz_l,
    rz_o,
    rz_l,
    all_new,
    local_sem,
    qz_send,
    qz_recv,
    qx_send,
    qx_recv,
    xo_send,
    xo_recv,
    xl_send,
    xl_recv,
    zo_send,
    zo_recv,
    zl_send,
    zl_recv,
    nz_send,
    nz_recv,
    nx_send,
    nx_recv,
    nh_send,
    nh_recv,
):
    rows, size = queries_ref.shape
    store_rows = keys_ref.shape[0]
    page = store_rows // slots
    new_tok = new_ref.shape[0] // 2
    scale = math.log2(math.e) / math.sqrt(size)
    store = lax.axis_index("ctx")
    head = lax.axis_index("head")
    z = lax.div(store, 2)
    x = lax.rem(store, 2)
    pair = store + 1 - 2 * x

    def along_z(steps):
        return 2 * lax.rem(z + steps, layers) + x

    def along_head(steps):
        return lax.rem(head + steps, heads_axis)

    load_q = pltpu.make_async_copy(queries_ref, qz_ref.at[0], local_sem.at[0])
    load_k = pltpu.make_async_copy(keys_ref, k_ref, local_sem.at[1])
    load_v = pltpu.make_async_copy(values_ref, v_ref.at[:, pl.ds(0, size)], local_sem.at[2])
    load_q.start()
    load_k.start()
    load_v.start()

    barrier = pltpu.get_barrier_semaphore()
    for steps in range(1, layers):
        pl.semaphore_signal(barrier, inc=1, device_id={"ctx": along_z(steps)}, device_id_type=MESH)
    pl.semaphore_signal(barrier, inc=1, device_id={"ctx": pair}, device_id_type=MESH)
    for steps in range(1, heads_axis):
        pl.semaphore_signal(
            barrier, inc=1, device_id={"head": along_head(steps)}, device_id_type=MESH
        )

    out_row = lax.broadcasted_iota(jnp.int32, (2 * new_tok, 2 * new_tok), 0)
    in_row = lax.broadcasted_iota(jnp.int32, (2 * new_tok, 2 * new_tok), 1)
    wanted = jnp.where(out_row < new_tok, 2 * out_row, 2 * (out_row - new_tok) + 1)
    order = jnp.where(in_row == wanted, 1.0, 0.0).astype(jnp.bfloat16)
    all_new[z, x, head] = jnp.dot(
        order, new_ref[...], preferred_element_type=jnp.float32
    ).astype(jnp.bfloat16)
    v_ref[:, pl.ds(size, size)] = jnp.ones((store_rows, size), jnp.bfloat16)

    pl.semaphore_wait(barrier, layers + heads_axis - 1)

    def remote(src, dst, send_sem, recv_sem, device):
        return pltpu.make_async_remote_copy(
            src_ref=src,
            dst_ref=dst,
            send_sem=send_sem,
            recv_sem=recv_sem,
            device_id=device,
            device_id_type=MESH,
        )

    def send_q(steps):
        slot = layers - steps
        return remote(
            queries_ref,
            qz_ref.at[slot],
            qz_send.at[steps],
            qz_recv.at[slot],
            {"ctx": along_z(steps)},
        )

    def take_q(slot):
        return remote(
            queries_ref, qz_ref.at[slot], qz_send.at[slot], qz_recv.at[slot], {"ctx": along_z(slot)}
        )

    def pass_q(slot):
        return remote(
            qz_ref.at[slot], qx_ref.at[slot], qx_send.at[slot], qx_recv.at[slot], {"ctx": pair}
        )

    first_pass = remote(
        queries_ref, qx_ref.at[0], qx_send.at[0], qx_recv.at[0], {"ctx": pair}
    )

    def cross(slot):
        return (
            remote(sx_o.at[slot], rx_o.at[slot], xo_send.at[slot], xo_recv.at[slot], {"ctx": pair}),
            remote(sx_l.at[slot], rx_l.at[slot], xl_send.at[slot], xl_recv.at[slot], {"ctx": pair}),
        )

    def give_back(steps):
        slot = layers - steps
        device = {"ctx": along_z(steps)}
        return (
            remote(sz_o.at[steps], rz_o.at[slot], zo_send.at[steps], zo_recv.at[slot], device),
            remote(sz_l.at[steps], rz_l.at[slot], zl_send.at[steps], zl_recv.at[slot], device),
        )

    def get_back(slot):
        device = {"ctx": along_z(slot)}
        return (
            remote(sz_o.at[slot], rz_o.at[slot], zo_send.at[slot], zo_recv.at[slot], device),
            remote(sz_l.at[slot], rz_l.at[slot], zl_send.at[slot], zl_recv.at[slot], device),
        )

    def new_z(steps):
        mine = all_new.at[z, x, head]
        return remote(
            mine, mine, nz_send.at[steps], nz_recv.at[layers - steps], {"ctx": along_z(steps)}
        )

    def new_z_taken(slot):
        theirs = all_new.at[lax.rem(z + slot, layers), x, head]
        return remote(theirs, theirs, nz_send.at[slot], nz_recv.at[slot], {"ctx": along_z(slot)})

    def new_x(parity):
        block = all_new.at[:, parity, head]
        return remote(block, block, nx_send, nx_recv, {"ctx": pair})

    def new_h(steps):
        mine = all_new.at[:, :, head]
        return remote(
            mine,
            mine,
            nh_send.at[steps],
            nh_recv.at[heads_axis - steps],
            {"head": along_head(steps)},
        )

    def new_h_taken(slot):
        theirs = all_new.at[:, :, along_head(slot)]
        return remote(
            theirs, theirs, nh_send.at[slot], nh_recv.at[slot], {"head": along_head(slot)}
        )

    first_pass.start()
    for steps in range(1, layers):
        send_q(steps).start()
    for steps in range(1, layers):
        new_z(steps).start()

    dead = []
    for number in range(slots):
        live = jnp.int32(0)
        for place in range(slots):
            hit = (table_ref[0, place] == number) & (place < count_ref[0])
            live = jnp.where(hit, jnp.int32(1), live)
        dead.append(jnp.where(live == 1, jnp.float32(0.0), jnp.float32(FAR)))

    def partial(query_rows):
        scores, top = [], None
        for number in range(slots):
            found = lax.dot_general(
                query_rows,
                k_ref[pl.ds(number * page, page), :],
                NT,
                preferred_element_type=jnp.float32,
            )
            scores.append(found)
            page_top = jnp.max(found, axis=1, keepdims=True) - dead[number]
            top = page_top if top is None else jnp.maximum(top, page_top)
        summed = None
        for number in range(slots):
            weights = jnp.exp2((scores[number] - (top + dead[number])) * scale)
            product = jnp.dot(
                weights.astype(jnp.bfloat16),
                v_ref[pl.ds(number * page, page), :],
                preferred_element_type=jnp.float32,
            )
            summed = product if summed is None else summed + product
        totals = summed[:, size:]
        level = top * scale + jnp.log2(totals)
        return summed[:, :size] / totals, level

    def write(mean, level, mean_ref, level_ref):
        largest = jnp.max(jnp.abs(mean), axis=1, keepdims=True)
        steps = jnp.round(mean * (STEPS / jnp.maximum(largest, TINY)))
        mean_ref[...] = steps.astype(jnp.int32).astype(jnp.int16)
        lane = lax.broadcasted_iota(jnp.int32, (rows, size), 1)
        level_ref[...] = jnp.where(lane == 0, level, largest * (1.0 / STEPS)).T[:8, :]

    def read(mean_ref, level_ref):
        level = jnp.broadcast_to(level_ref[0:1, :], (size, rows)).T
        step = jnp.broadcast_to(level_ref[1:2, :], (size, rows)).T
        return mean_ref[...].astype(jnp.int32).astype(jnp.float32) * step, level

    def merged(parts):
        top = functools.reduce(jnp.maximum, [level for _, level in parts])
        share = [jnp.exp2(level - top) for _, level in parts]
        whole = functools.reduce(jnp.add, share)
        summed = functools.reduce(jnp.add, [one * mean for one, (mean, _) in zip(share, parts)])
        return summed / whole, top + jnp.log2(whole)

    def join_pair(slot):
        for copy in cross(slot):
            copy.wait_recv()
        return merged(
            [
                (own_o[slot], own_l[slot]),
                read(rx_o.at[slot], rx_l.at[slot]),
            ]
        )

    def send_joined(slot):
        mean, level = join_pair(slot)
        write(mean, level, sz_o.at[slot], sz_l.at[slot])
        for copy in give_back(slot):
            copy.start()

    def serve_pair(slot):
        mean, level = partial(qx_ref[slot])
        write(mean, level, sx_o.at[slot], sx_l.at[slot])
        for copy in cross(slot):
            copy.start()

    load_q.wait()
    load_k.wait()
    load_v.wait()
    mean, level = partial(qz_ref[0])
    own_o[0] = mean
    own_l[0] = level

    def layer_step(slot, carry):
        take_q(slot).wait_recv()
        pass_q(slot).start()
        mean, level = partial(qz_ref[slot])
        own_o[slot] = mean
        own_l[slot] = level
        pass_q(slot).wait_recv()
        serve_pair(slot)

        @pl.when(slot == 1)
        def _():
            for other in range(1, layers):
                new_z_taken(other).wait_recv()
            new_x(x).start()

        @pl.when(slot >= 2)
        def _():
            send_joined(slot - 1)

        @pl.when(slot == 2)
        def _():
            new_x(1 - x).wait_recv()
            for steps in range(1, heads_axis):
                new_h(steps).start()

        return carry

    lax.fori_loop(1, layers, layer_step, 0)
    first_pass.wait_recv()
    serve_pair(0)
    send_joined(layers - 1)

    for slot in range(1, heads_axis):
        new_h_taken(slot).wait_recv()
    tokens = layers * 2 * heads_axis * new_tok
    gathered = all_new[...].astype(jnp.float32).reshape(tokens // new_tok, 2, new_tok, size)
    new_keys = gathered[:, 0].reshape(tokens, size).astype(jnp.bfloat16)
    new_values = gathered[:, 1].reshape(tokens, size).astype(jnp.bfloat16)

    mine = owner_ref[...] == store
    target = jnp.where(mine, 2 * offset_ref[...], -2)
    place = lax.broadcasted_iota(jnp.int32, (appended_ref.shape[0], tokens), 0)
    key_rows = jnp.where(place == target, 1.0, 0.0).astype(jnp.bfloat16)
    value_rows = jnp.where(place == target + 1, 1.0, 0.0).astype(jnp.bfloat16)
    appended_ref[...] = (
        jnp.dot(key_rows, new_keys, preferred_element_type=jnp.float32)
        + jnp.dot(value_rows, new_values, preferred_element_type=jnp.float32)
    ).astype(jnp.bfloat16)

    scores = lax.dot_general(qz_ref[0], new_keys, NT, preferred_element_type=jnp.float32)
    column = lax.broadcasted_iota(jnp.int32, (1, tokens), 1) * head_dev - store * rows
    row = lax.broadcasted_iota(jnp.int32, (rows, tokens), 0)
    scores = jnp.where(column <= row, scores, -FAR)
    top = jnp.max(scores, axis=1, keepdims=True)
    weights = jnp.exp2((scores - top) * scale)
    totals = jnp.sum(weights, axis=1, keepdims=True)
    summed = jnp.dot(weights.astype(jnp.bfloat16), new_values, preferred_element_type=jnp.float32)
    self_level = jnp.broadcast_to(top * scale + jnp.log2(totals), (rows, size))
    parts = [(summed / totals, self_level), join_pair(0)]
    for slot in range(1, layers):
        for copy in get_back(slot):
            copy.wait_recv()
        parts.append(read(rz_o.at[slot], rz_l.at[slot]))
    attended_ref[...] = merged(parts)[0].astype(jnp.bfloat16)

    first_pass.wait_send()
    for slot in range(layers):
        for copy in cross(slot):
            copy.wait_send()
        if slot:
            send_q(slot).wait_send()
            pass_q(slot).wait_send()
            new_z(slot).wait_send()
            for copy in give_back(slot):
                copy.wait_send()
    new_x(x).wait_send()
    for steps in range(1, heads_axis):
        new_h(steps).wait_send()


def shards(
    queries, cache_keys, cache_values, page_table, page_count, new_kv, new_owner, new_offset
):
    tok_dev, head_dev, size = queries.shape
    new_tok = new_kv.shape[0]
    slots = page_table.shape[1]
    store_rows = cache_keys.shape[0]
    stores = lax.axis_size("ctx")
    heads_axis = lax.axis_size("head")
    layers = stores // 2
    rows = tok_dev * head_dev
    append_rows = 2 * tok_dev
    tokens = new_owner.shape[0]
    bf16, f32 = jnp.bfloat16, jnp.float32
    vmem = pl.BlockSpec(memory_space=pltpu.VMEM)
    smem = pl.BlockSpec(memory_space=pltpu.SMEM)
    anywhere = pl.BlockSpec(memory_space=pl.ANY)
    mean_block = pltpu.VMEM((layers, rows, size), bf16)
    part_block = pltpu.VMEM((layers, rows, size), jnp.int16)
    level_block = pltpu.VMEM((layers, 8, rows), f32)
    dma = pltpu.SemaphoreType.DMA((layers,))
    attended, appended = pl.pallas_call(
        functools.partial(attention_kernel, layers, heads_axis, head_dev, slots),
        out_shape=(
            jax.ShapeDtypeStruct((rows, size), bf16),
            jax.ShapeDtypeStruct((2 * append_rows, size), bf16),
        ),
        in_specs=[smem, smem, anywhere, anywhere, anywhere, vmem, vmem, vmem],
        out_specs=(vmem, vmem),
        scratch_shapes=[
            pltpu.VMEM((store_rows, size), bf16),
            pltpu.VMEM((store_rows, 2 * size), bf16),
            mean_block,
            mean_block,
            pltpu.VMEM((layers, rows, size), f32),
            pltpu.VMEM((layers, rows, size), f32),
            part_block,
            level_block,
            part_block,
            level_block,
            part_block,
            level_block,
            part_block,
            level_block,
            pltpu.VMEM((layers, 2, heads_axis, 2 * new_tok, size), bf16),
            pltpu.SemaphoreType.DMA((3,)),
        ]
        + [dma] * 14
        + [
            pltpu.SemaphoreType.DMA,
            pltpu.SemaphoreType.DMA,
            pltpu.SemaphoreType.DMA((heads_axis,)),
            pltpu.SemaphoreType.DMA((heads_axis,)),
        ],
        compiler_params=pltpu.CompilerParams(
            collective_id=0, has_side_effects=True, vmem_limit_bytes=40 * 1024 * 1024
        ),
    )(
        page_table,
        page_count,
        queries.reshape(rows, size),
        cache_keys,
        cache_values,
        new_kv.reshape(2 * new_tok, size),
        new_owner.reshape(1, tokens),
        new_offset.reshape(1, tokens),
    )
    return (
        attended.reshape(tok_dev, head_dev, size),
        appended.reshape(append_rows, 2, size),
    )


def solution(mesh):
    in_specs = (
        P("ctx", "head", None),
        P("ctx", None),
        P("ctx", None),
        P("ctx", None),
        P("ctx"),
        P(("ctx", "head"), None, None),
        P(),
        P(),
    )
    out_specs = (P("ctx", "head", None), P("ctx", None, None))
    return jax.shard_map(shards, mesh=mesh, in_specs=in_specs, out_specs=out_specs, check_vma=False)
```

time: 276 us -> 45.3 us (0.16)
  starting transfers between devices: 81.5 us -> 0 us
  waiting for transfers between devices: 54.7 us -> 0 us
  blocking collectives: 39.6 us -> 0 us
  matrix products: 38.7 us -> 0 us
  Pallas kernels: 0 us -> 37.4 us
  loops' own time: 26.8 us -> 0 us
  local copies, waits for them, and re-layouts: 30.9 us -> 6.19 us
  other arithmetic: 4.4 us -> 0 us
    ppermute x32 -> x0, starting transfers between devices: 81.5 us -> none  [passed_along(): return lax.ppermute(value, axis, pairs)]
    ppermute x32 -> x0, waiting for transfers between devices: 54.7 us -> none  [passed_along(): return lax.ppermute(value, axis, pairs)]
    all_gather x1 -> x0, blocking collectives: 39.6 us -> none  [shards(): new_rows = lax.all_gather(new_kv, ('ctx', 'head'), axis=0, tiled=True)]
    dot_general x34 -> x0, matrix products: 38.7 us -> none  [the longest x16 19.4 us: take_page(): jnp.dot(weights.astype(jnp.bfloat16), value_block, preferred_element_type...]
    pallas_call x0 -> x1, Pallas kernels: none -> 37.4 us  [shards(): pl.pallas_call(functools.partial(attention_kernel, layers, heads_axis, he...]
    another operation x9 -> x0, loops' own time: 26.8 us -> none  [the longest x8 26.2 us: cache_part(): return lax.fori_loop(0, live_count, take_page, initial)]
    scatter x1 -> x0, local copies, waits for them, and re-layouts: 15.4 us -> none  [shards(): jnp.zeros((append_rows, 2, head_size), jnp.bfloat16).at[target]]
    dynamic_slice x16 -> x0, local copies, waits for them, and re-layouts: 9.53 us -> none  [take_page(): page_index = lax.dynamic_index_in_dim(table_row, number, 0, keepdims=False)]
  transfers between devices with their start and end apart: 32 -> 0, of which waited for: 16 -> 0; matrix products, arithmetic and copies ran while one was open for 0% -> 0% of each run, Pallas kernels for 0% -> 0%
where the time goes in v1:
time: 45.3 us; the launch traced here: 44.9 us
  Pallas kernels  37.4 us (83%)
  local copies, waits for them, and re-layouts  6.19 us (14%)
  between operations  1.32 us (3%)
    pallas_call x1, Pallas kernels, shards(): pl.pallas_call(functools.partial(attention_kernel, layers, heads_axis, he...  37.4 us
    unnamed x16, local copies, waits for them, and re-layouts  6.19 us

profile of v1, /device:TPU:0, one launch (start us, length us, event | category | flops | bytes accessed | tf_op | source)
XLA Modules:
  0.0 44.9 jit_solution(6560612132255634714)
XLA Ops:
  0.6 0.0 copy-start.3
  1.3 0.0 copy-start.6
  1.3 0.0 copy-done.3
  1.3 0.6 %copy-done.6 = s32[1,4]{1,0:T(1,128)S(1)} copy-done((s32[1,4]{1,0:T(1,128)S(1)}, s32[1,4]{1,0:T(1,128)}, u32[]{:S(2)}) %copy-start.6) | copy-done | bytes 40
  2.0 0.0 copy-start
  2.0 1.0 %copy-done = bf16[2048,128]{1,0:T(8,128)(2,1)S(1)} copy-done((bf16[2048,128]{1,0:T(8,128)(2,1)S(1)}, bf16[2048,128]{1,0:T(8,128)(2,1)}, u32[]{:S(2)}) %copy-start) | copy-done | bytes 524312
  3.0 0.0 copy-start.1
  3.0 1.0 %copy-done.1 = bf16[2048,128]{1,0:T(8,128)(2,1)S(1)} copy-done((bf16[2048,128]{1,0:T(8,128)(2,1)S(1)}, bf16[2048,128]{1,0:T(8,128)(2,1)}, u32[]{:S(2)}) %copy-start.1) | copy-done | bytes 524312
  4.0 0.0 copy-start.2
  4.0 0.8 %copy-done.2 = bf16[64,4,128]{2,1,0:T(4,128)(2,1)S(1)} copy-done((bf16[64,4,128]{2,1,0:T(4,128)(2,1)S(1)}, bf16[64,4,128]{2,1,0:T(4,128)(2,1)}, u32[]{:S(2)}) %copy-start.2) | copy-done | bytes 65560
  4.9 0.0 copy-start.4
  4.9 0.7 %copy-done.4 = s32[512]{0:T(512)S(1)} copy-done((s32[512]{0:T(512)S(1)}, s32[512]{0:T(512)}, u32[]{:S(2)}) %copy-start.4) | copy-done | bytes 2072
  5.6 0.0 copy-start.5
  5.6 0.7 %copy-done.5 = s32[512]{0:T(512)S(1)} copy-done((s32[512]{0:T(512)S(1)}, s32[512]{0:T(512)}, u32[]{:S(2)}) %copy-start.5) | copy-done | bytes 2072
  6.2 37.4 %shard_map.95 = (bf16[256,128]{1,0:T(8,128)(2,1)S(1)}, bf16[256,128]{1,0:T(8,128)(2,1)S(1)}) custom-call(s32[1,4]{1,0:T(1,128)S(1)} %copy-done.6, s32[1]{0:T(128)S(6)} %copy.12.count_ref, bf16[256,128]{1,0:T(8,128)(2,1)S(1)} %bitcast.6, bf16[2048,128]{1,0:T(8,128)(2,1)S(1)} %copy-done, bf16[2048,128]{1,0:T(8,128)(2,1)S(1)} %copy-done.1, ...), custom_call_target="tpu_custom_call" | custom-call | tf_op jit(solution)/shard_map/pallas_call | solution.py:385
  43.7 0.6 %copy.13 = bf16[64,4,128]{2,1,0:T(4,128)(2,1)} copy(bf16[64,4,128]{2,1,0:T(4,128)(2,1)S(1)} %bitcast.8) | data formatting | bytes 131072
  44.3 0.6 %copy.14 = bf16[128,2,128]{2,1,0:T(2,128)(2,1)} copy(bf16[128,2,128]{2,1,0:T(2,128)(2,1)S(1)} %bitcast.7) | data formatting | bytes 131072
Async XLA Ops:
  0.6 0.7 %copy-start.3 = (bf16[16,2,128]{2,1,0:T(2,128)(2,1)S(1)}, bf16[16,2,128]{2,1,0:T(2,128)(2,1)}, u32[]{:S(2)}) copy-start(bf16[16,2,128]{2,1,0:T(2,128)(2,1)} %param.13) | copy-start | bytes 24580
  1.3 0.7 %copy-start.6 = (s32[1,4]{1,0:T(1,128)S(1)}, s32[1,4]{1,0:T(1,128)}, u32[]{:S(2)}) copy-start(s32[1,4]{1,0:T(1,128)} %table_ref.1) | copy-start | bytes 52
  2.0 1.0 %copy-start = (bf16[2048,128]{1,0:T(8,128)(2,1)S(1)}, bf16[2048,128]{1,0:T(8,128)(2,1)}, u32[]{:S(2)}) copy-start(bf16[2048,128]{1,0:T(8,128)(2,1)} %keys_ref.1) | copy-start | bytes 1572868
  3.0 1.0 %copy-start.1 = (bf16[2048,128]{1,0:T(8,128)(2,1)S(1)}, bf16[2048,128]{1,0:T(8,128)(2,1)}, u32[]{:S(2)}) copy-start(bf16[2048,128]{1,0:T(8,128)(2,1)} %values_ref.1) | copy-start | bytes 1572868
  4.0 0.8 %copy-start.2 = (bf16[64,4,128]{2,1,0:T(4,128)(2,1)S(1)}, bf16[64,4,128]{2,1,0:T(4,128)(2,1)}, u32[]{:S(2)}) copy-start(bf16[64,4,128]{2,1,0:T(4,128)(2,1)} %param.8) | copy-start | bytes 196612
  4.9 0.7 %copy-start.4 = (s32[512]{0:T(512)S(1)}, s32[512]{0:T(512)}, u32[]{:S(2)}) copy-start(s32[512]{0:T(512)} %param.14) | copy-start | bytes 6148
  5.6 0.7 %copy-start.5 = (s32[512]{0:T(512)S(1)}, s32[512]{0:T(512)}, u32[]{:S(2)}) copy-start(s32[512]{0:T(512)} %param.15) | copy-start | bytes 6148

commit v2 on v1

--- a/solution.py
+++ b/solution.py
@@ -20,17 +20,22 @@
     heads_axis,
     head_dev,
     slots,
-    table_ref,
+    table_hbm,
     count_ref,
     queries_ref,
     keys_ref,
     values_ref,
+    new_hbm,
+    owner_hbm,
+    offset_hbm,
+    attended_ref,
+    appended_ref,
+    table_ref,
     new_ref,
     owner_ref,
     offset_ref,
-    attended_ref,
-    appended_ref,
     k_ref,
+    kt_ref,
     v_ref,
     qz_ref,
     qx_ref,
@@ -68,7 +73,7 @@
     rows, size = queries_ref.shape
     store_rows = keys_ref.shape[0]
     page = store_rows // slots
-    new_tok = new_ref.shape[0] // 2
+    new_tok = new_hbm.shape[0] // 2
     scale = math.log2(math.e) / math.sqrt(size)
     store = lax.axis_index("ctx")
     head = lax.axis_index("head")
@@ -82,12 +87,21 @@
     def along_head(steps):
         return lax.rem(head + steps, heads_axis)
 
+    load_new = pltpu.make_async_copy(new_hbm, new_ref, local_sem.at[3])
+    small = [
+        pltpu.make_async_copy(table_hbm, table_ref, local_sem.at[4]),
+        pltpu.make_async_copy(owner_hbm, owner_ref, local_sem.at[5]),
+        pltpu.make_async_copy(offset_hbm, offset_ref, local_sem.at[6]),
+    ]
     load_q = pltpu.make_async_copy(queries_ref, qz_ref.at[0], local_sem.at[0])
     load_k = pltpu.make_async_copy(keys_ref, k_ref, local_sem.at[1])
     load_v = pltpu.make_async_copy(values_ref, v_ref.at[:, pl.ds(0, size)], local_sem.at[2])
+    load_new.start()
+    load_k.start()
     load_q.start()
-    load_k.start()
     load_v.start()
+    for load in small:
+        load.start()
 
     barrier = pltpu.get_barrier_semaphore()
     for steps in range(1, layers):
@@ -102,6 +116,7 @@
     in_row = lax.broadcasted_iota(jnp.int32, (2 * new_tok, 2 * new_tok), 1)
     wanted = jnp.where(out_row < new_tok, 2 * out_row, 2 * (out_row - new_tok) + 1)
     order = jnp.where(in_row == wanted, 1.0, 0.0).astype(jnp.bfloat16)
+    load_new.wait()
     all_new[z, x, head] = jnp.dot(
         order, new_ref[...], preferred_element_type=jnp.float32
     ).astype(jnp.bfloat16)
@@ -200,6 +215,8 @@
     for steps in range(1, layers):
         new_z(steps).start()
 
+    for load in small:
+        load.wait()
     dead = []
     for number in range(slots):
         live = jnp.int32(0)
@@ -211,10 +228,9 @@
     def partial(query_rows):
         scores, top = [], None
         for number in range(slots):
-            found = lax.dot_general(
+            found = jnp.dot(
                 query_rows,
-                k_ref[pl.ds(number * page, page), :],
-                NT,
+                kt_ref[:, pl.ds(number * page, page)],
                 preferred_element_type=jnp.float32,
             )
             scores.append(found)
@@ -274,19 +290,26 @@
         for copy in cross(slot):
             copy.start()
 
+    load_k.wait()
+    kt_ref[...] = k_ref[...].T
     load_q.wait()
-    load_k.wait()
     load_v.wait()
     mean, level = partial(qz_ref[0])
     own_o[0] = mean
     own_l[0] = level
+    take_q(1).wait_recv()
+    pass_q(1).start()
 
     def layer_step(slot, carry):
-        take_q(slot).wait_recv()
-        pass_q(slot).start()
         mean, level = partial(qz_ref[slot])
         own_o[slot] = mean
         own_l[slot] = level
+
+        @pl.when(slot < layers - 1)
+        def _():
+            take_q(slot + 1).wait_recv()
+            pass_q(slot + 1).start()
+
         pass_q(slot).wait_recv()
         serve_pair(slot)
 
@@ -377,7 +400,7 @@
     bf16, f32 = jnp.bfloat16, jnp.float32
     vmem = pl.BlockSpec(memory_space=pltpu.VMEM)
     smem = pl.BlockSpec(memory_space=pltpu.SMEM)
-    anywhere = pl.BlockSpec(memory_space=pl.ANY)
+    hbm = pl.BlockSpec(memory_space=pltpu.HBM)
     mean_block = pltpu.VMEM((layers, rows, size), bf16)
     part_block = pltpu.VMEM((layers, rows, size), jnp.int16)
     level_block = pltpu.VMEM((layers, 8, rows), f32)
@@ -388,10 +411,15 @@
             jax.ShapeDtypeStruct((rows, size), bf16),
             jax.ShapeDtypeStruct((2 * append_rows, size), bf16),
         ),
-        in_specs=[smem, smem, anywhere, anywhere, anywhere, vmem, vmem, vmem],
+        in_specs=[hbm, smem] + [hbm] * 6,
         out_specs=(vmem, vmem),
         scratch_shapes=[
+            pltpu.SMEM((1, slots), jnp.int32),
+            pltpu.VMEM((2 * new_tok, size), bf16),
+            pltpu.VMEM((1, tokens), jnp.int32),
+            pltpu.VMEM((1, tokens), jnp.int32),
             pltpu.VMEM((store_rows, size), bf16),
+            pltpu.VMEM((size, store_rows), bf16),
             pltpu.VMEM((store_rows, 2 * size), bf16),
             mean_block,
             mean_block,
@@ -406,7 +434,7 @@
             part_block,
             level_block,
             pltpu.VMEM((layers, 2, heads_axis, 2 * new_tok, size), bf16),
-            pltpu.SemaphoreType.DMA((3,)),
+            pltpu.SemaphoreType.DMA((7,)),
         ]
         + [dma] * 14
         + [
@@ -416,7 +444,7 @@
             pltpu.SemaphoreType.DMA((heads_axis,)),
         ],
         compiler_params=pltpu.CompilerParams(
-            collective_id=0, has_side_effects=True, vmem_limit_bytes=40 * 1024 * 1024
+            collective_id=0, has_side_effects=True, vmem_limit_bytes=62 * 1024 * 1024
         ),
     )(
         page_table,

time: 45.3 us -> 38.1 us (0.84)
  local copies, waits for them, and re-layouts: 6.19 us -> 2.16 us
  Pallas kernels: 37.4 us -> 34.5 us
    unnamed x16 -> x4, local copies, waits for them, and re-layouts: 6.19 us -> 2.16 us
    pallas_call x1, Pallas kernels: 37.4 us -> 34.5 us  [shards(): pl.pallas_call(functools.partial(attention_kernel, layers, heads_axis, he...]
where the time goes in v2:
time: 38.1 us; the launch traced here: 37.9 us
  Pallas kernels  34.5 us (91%)
  local copies, waits for them, and re-layouts  2.16 us (6%)
  between operations  1.29 us (3%)
    pallas_call x1, Pallas kernels, shards(): pl.pallas_call(functools.partial(attention_kernel, layers, heads_axis, he...  34.5 us
    unnamed x4, local copies, waits for them, and re-layouts  2.16 us

profile of v2, /device:TPU:0, one launch (start us, length us, event | category | flops | bytes accessed | tf_op | source)
XLA Modules:
  0.0 37.9 jit_solution(10647169772917314178)
XLA Ops:
  1.3 34.5 %shard_map.95 = (bf16[256,128]{1,0:T(8,128)(2,1)}, bf16[256,128]{1,0:T(8,128)(2,1)}) custom-call(s32[1,4]{1,0:T(1,128)} %table_hbm.1, s32[1]{0:T(128)S(6)} %copy.12.count_ref, bf16[256,128]{1,0:T(8,128)(2,1)} %bitcast.6, bf16[2048,128]{1,0:T(8,128)(2,1)} %keys_ref.1, bf16[2048,128]{1,0:T(8,128)(2,1)} %values_ref.1, bf16[32,128]{1,0:T(8,128)(2,1)} %bitcast.9, ...), custom_call_target="tpu_custom_call" | custom-call | tf_op jit(solution)/shard_map/pallas_call | solution.py:408
  35.7 0.0 copy-start
  35.8 1.5 %copy.13 = bf16[64,4,128]{2,1,0:T(4,128)(2,1)} copy(bf16[64,4,128]{2,1,0:T(4,128)(2,1)} %bitcast.8) | data formatting | bytes 131072
  37.3 0.0 copy-done
  37.3 0.6 %copy.14 = bf16[128,2,128]{2,1,0:T(2,128)(2,1)} copy(bf16[128,2,128]{2,1,0:T(2,128)(2,1)S(1)} %bitcast.7) | data formatting | bytes 131072
Async XLA Ops:
  35.7 1.5 %copy-start = (bf16[256,128]{1,0:T(8,128)(2,1)S(1)}, bf16[256,128]{1,0:T(8,128)(2,1)}, u32[]{:S(2)}) copy-start(bf16[256,128]{1,0:T(8,128)(2,1)} %get-tuple-element.5) | copy-start | bytes 196612

commit v3 on v2

--- a/solution.py
+++ b/solution.py
@@ -12,7 +12,6 @@
 FAR = 1e30
 STEPS = 32767.0
 TINY = 1e-30
-NT = (((1,), (1,)), ((), ()))
 
 
 def attention_kernel(
@@ -34,9 +33,10 @@
     new_ref,
     owner_ref,
     offset_ref,
+    q_ref,
     k_ref,
-    kt_ref,
     v_ref,
+    vt_ref,
     qz_ref,
     qx_ref,
     own_o,
@@ -93,12 +93,12 @@
         pltpu.make_async_copy(owner_hbm, owner_ref, local_sem.at[5]),
         pltpu.make_async_copy(offset_hbm, offset_ref, local_sem.at[6]),
     ]
-    load_q = pltpu.make_async_copy(queries_ref, qz_ref.at[0], local_sem.at[0])
+    load_q = pltpu.make_async_copy(queries_ref, q_ref, local_sem.at[0])
     load_k = pltpu.make_async_copy(keys_ref, k_ref, local_sem.at[1])
-    load_v = pltpu.make_async_copy(values_ref, v_ref.at[:, pl.ds(0, size)], local_sem.at[2])
+    load_v = pltpu.make_async_copy(values_ref, v_ref, local_sem.at[2])
+    load_q.start()
     load_new.start()
     load_k.start()
-    load_q.start()
     load_v.start()
     for load in small:
         load.start()
@@ -120,7 +120,8 @@
     all_new[z, x, head] = jnp.dot(
         order, new_ref[...], preferred_element_type=jnp.float32
     ).astype(jnp.bfloat16)
-    v_ref[:, pl.ds(size, size)] = jnp.ones((store_rows, size), jnp.bfloat16)
+    load_q.wait()
+    qz_ref[0] = q_ref[...].T
 
     pl.semaphore_wait(barrier, layers + heads_axis - 1)
 
@@ -137,7 +138,7 @@
     def send_q(steps):
         slot = layers - steps
         return remote(
-            queries_ref,
+            qz_ref.at[0],
             qz_ref.at[slot],
             qz_send.at[steps],
             qz_recv.at[slot],
@@ -146,7 +147,7 @@
 
     def take_q(slot):
         return remote(
-            queries_ref, qz_ref.at[slot], qz_send.at[slot], qz_recv.at[slot], {"ctx": along_z(slot)}
+            qz_ref.at[0], qz_ref.at[slot], qz_send.at[slot], qz_recv.at[slot], {"ctx": along_z(slot)}
         )
 
     def pass_q(slot):
@@ -155,7 +156,7 @@
         )
 
     first_pass = remote(
-        queries_ref, qx_ref.at[0], qx_send.at[0], qx_recv.at[0], {"ctx": pair}
+        qz_ref.at[0], qx_ref.at[0], qx_send.at[0], qx_recv.at[0], {"ctx": pair}
     )
 
     def cross(slot):
@@ -225,41 +226,39 @@
             live = jnp.where(hit, jnp.int32(1), live)
         dead.append(jnp.where(live == 1, jnp.float32(0.0), jnp.float32(FAR)))
 
-    def partial(query_rows):
+    def partial(query_columns):
         scores, top = [], None
         for number in range(slots):
             found = jnp.dot(
-                query_rows,
-                kt_ref[:, pl.ds(number * page, page)],
+                k_ref[pl.ds(number * page, page), :],
+                query_columns,
                 preferred_element_type=jnp.float32,
             )
             scores.append(found)
-            page_top = jnp.max(found, axis=1, keepdims=True) - dead[number]
+            page_top = jnp.max(found, axis=0, keepdims=True) - dead[number]
             top = page_top if top is None else jnp.maximum(top, page_top)
         summed = None
         for number in range(slots):
             weights = jnp.exp2((scores[number] - (top + dead[number])) * scale)
             product = jnp.dot(
+                vt_ref[:, pl.ds(number * page, page)],
                 weights.astype(jnp.bfloat16),
-                v_ref[pl.ds(number * page, page), :],
                 preferred_element_type=jnp.float32,
             )
             summed = product if summed is None else summed + product
-        totals = summed[:, size:]
-        level = top * scale + jnp.log2(totals)
-        return summed[:, :size] / totals, level
+        totals = summed[size : size + 1, :]
+        return summed[:size, :] / totals, top * scale + jnp.log2(totals)
 
     def write(mean, level, mean_ref, level_ref):
-        largest = jnp.max(jnp.abs(mean), axis=1, keepdims=True)
+        largest = jnp.max(jnp.abs(mean), axis=0, keepdims=True)
         steps = jnp.round(mean * (STEPS / jnp.maximum(largest, TINY)))
         mean_ref[...] = steps.astype(jnp.int32).astype(jnp.int16)
-        lane = lax.broadcasted_iota(jnp.int32, (rows, size), 1)
-        level_ref[...] = jnp.where(lane == 0, level, largest * (1.0 / STEPS)).T[:8, :]
+        line = lax.broadcasted_iota(jnp.int32, (8, rows), 0)
+        level_ref[...] = jnp.where(line == 0, level, largest * (1.0 / STEPS))
 
     def read(mean_ref, level_ref):
-        level = jnp.broadcast_to(level_ref[0:1, :], (size, rows)).T
-        step = jnp.broadcast_to(level_ref[1:2, :], (size, rows)).T
-        return mean_ref[...].astype(jnp.int32).astype(jnp.float32) * step, level
+        step = level_ref[1:2, :]
+        return mean_ref[...].astype(jnp.int32).astype(jnp.float32) * step, level_ref[0:1, :]
 
     def merged(parts):
         top = functools.reduce(jnp.maximum, [level for _, level in parts])
@@ -273,7 +272,7 @@
             copy.wait_recv()
         return merged(
             [
-                (own_o[slot], own_l[slot]),
+                (own_o[slot], own_l[slot, 0:1, :]),
                 read(rx_o.at[slot], rx_l.at[slot]),
             ]
         )
@@ -291,19 +290,19 @@
             copy.start()
 
     load_k.wait()
-    kt_ref[...] = k_ref[...].T
-    load_q.wait()
     load_v.wait()
+    vt_ref[pl.ds(0, size), :] = v_ref[...].T
+    vt_ref[pl.ds(size, 16), :] = jnp.ones((16, store_rows), jnp.bfloat16)
     mean, level = partial(qz_ref[0])
     own_o[0] = mean
-    own_l[0] = level
+    own_l[0, 0:1, :] = level
     take_q(1).wait_recv()
     pass_q(1).start()
 
     def layer_step(slot, carry):
         mean, level = partial(qz_ref[slot])
         own_o[slot] = mean
-        own_l[slot] = level
+        own_l[slot, 0:1, :] = level
 
         @pl.when(slot < layers - 1)
         def _():
@@ -353,21 +352,22 @@
         + jnp.dot(value_rows, new_values, preferred_element_type=jnp.float32)
     ).astype(jnp.bfloat16)
 
-    scores = lax.dot_general(qz_ref[0], new_keys, NT, preferred_element_type=jnp.float32)
-    column = lax.broadcasted_iota(jnp.int32, (1, tokens), 1) * head_dev - store * rows
-    row = lax.broadcasted_iota(jnp.int32, (rows, tokens), 0)
-    scores = jnp.where(column <= row, scores, -FAR)
-    top = jnp.max(scores, axis=1, keepdims=True)
+    scores = jnp.dot(new_keys, qz_ref[0], preferred_element_type=jnp.float32)
+    token = lax.broadcasted_iota(jnp.int32, (tokens, rows), 0)
+    asker = lax.broadcasted_iota(jnp.int32, (tokens, rows), 1)
+    scores = jnp.where(token * head_dev - store * rows <= asker, scores, -FAR)
+    top = jnp.max(scores, axis=0, keepdims=True)
     weights = jnp.exp2((scores - top) * scale)
-    totals = jnp.sum(weights, axis=1, keepdims=True)
-    summed = jnp.dot(weights.astype(jnp.bfloat16), new_values, preferred_element_type=jnp.float32)
-    self_level = jnp.broadcast_to(top * scale + jnp.log2(totals), (rows, size))
-    parts = [(summed / totals, self_level), join_pair(0)]
+    totals = jnp.sum(weights, axis=0, keepdims=True)
+    summed = jnp.dot(
+        new_values.T, weights.astype(jnp.bfloat16), preferred_element_type=jnp.float32
+    )
+    parts = [(summed / totals, top * scale + jnp.log2(totals)), join_pair(0)]
     for slot in range(1, layers):
         for copy in get_back(slot):
             copy.wait_recv()
         parts.append(read(rz_o.at[slot], rz_l.at[slot]))
-    attended_ref[...] = merged(parts)[0].astype(jnp.bfloat16)
+    attended_ref[...] = merged(parts)[0].T.astype(jnp.bfloat16)
 
     first_pass.wait_send()
     for slot in range(layers):
@@ -401,8 +401,8 @@
     vmem = pl.BlockSpec(memory_space=pltpu.VMEM)
     smem = pl.BlockSpec(memory_space=pltpu.SMEM)
     hbm = pl.BlockSpec(memory_space=pltpu.HBM)
-    mean_block = pltpu.VMEM((layers, rows, size), bf16)
-    part_block = pltpu.VMEM((layers, rows, size), jnp.int16)
+    mean_block = pltpu.VMEM((layers, size, rows), bf16)
+    part_block = pltpu.VMEM((layers, size, rows), jnp.int16)
     level_block = pltpu.VMEM((layers, 8, rows), f32)
     dma = pltpu.SemaphoreType.DMA((layers,))
     attended, appended = pl.pallas_call(
@@ -418,13 +418,14 @@
             pltpu.VMEM((2 * new_tok, size), bf16),
             pltpu.VMEM((1, tokens), jnp.int32),
             pltpu.VMEM((1, tokens), jnp.int32),
+            pltpu.VMEM((rows, size), bf16),
             pltpu.VMEM((store_rows, size), bf16),
-            pltpu.VMEM((size, store_rows), bf16),
-            pltpu.VMEM((store_rows, 2 * size), bf16),
+            pltpu.VMEM((store_rows, size), bf16),
+            pltpu.VMEM((size + 16, store_rows), bf16),
             mean_block,
             mean_block,
-            pltpu.VMEM((layers, rows, size), f32),
-            pltpu.VMEM((layers, rows, size), f32),
+            pltpu.VMEM((layers, size, rows), f32),
+            level_block,
             part_block,
             level_block,
             part_block,

time: 38.1 us -> 36.9 us (0.969)
  Pallas kernels: 34.5 us -> 33.2 us
    pallas_call x1, Pallas kernels: 34.5 us -> 33.2 us  [shards(): pl.pallas_call(functools.partial(attention_kernel, layers, heads_axis, he...]
where the time goes in v3:
time: 36.9 us; the launch traced here: 36.7 us
  Pallas kernels  33.2 us (90%)
  local copies, waits for them, and re-layouts  2.16 us (6%)
  between operations  1.29 us (3%)
    pallas_call x1, Pallas kernels, shards(): pl.pallas_call(functools.partial(attention_kernel, layers, heads_axis, he...  33.2 us
    unnamed x4, local copies, waits for them, and re-layouts  2.16 us

profile of v3, /device:TPU:0, one launch (start us, length us, event | category | flops | bytes accessed | tf_op | source)
XLA Modules:
  0.0 36.7 jit_solution(16397193395679229667)
XLA Ops:
  1.3 33.2 %shard_map.95 = (bf16[256,128]{1,0:T(8,128)(2,1)}, bf16[256,128]{1,0:T(8,128)(2,1)}) custom-call(s32[1,4]{1,0:T(1,128)} %table_hbm.1, s32[1]{0:T(128)S(6)} %copy.12.count_ref, bf16[256,128]{1,0:T(8,128)(2,1)} %bitcast.6, bf16[2048,128]{1,0:T(8,128)(2,1)} %keys_ref.1, bf16[2048,128]{1,0:T(8,128)(2,1)} %values_ref.1, bf16[32,128]{1,0:T(8,128)(2,1)} %bitcast.9, ...), custom_call_target="tpu_custom_call" | custom-call | tf_op jit(solution)/shard_map/pallas_call | solution.py:408
  34.5 0.0 copy-start
  34.5 1.5 %copy.13 = bf16[64,4,128]{2,1,0:T(4,128)(2,1)} copy(bf16[64,4,128]{2,1,0:T(4,128)(2,1)} %bitcast.8) | data formatting | bytes 131072
  36.1 0.0 copy-done
  36.1 0.6 %copy.14 = bf16[128,2,128]{2,1,0:T(2,128)(2,1)} copy(bf16[128,2,128]{2,1,0:T(2,128)(2,1)S(1)} %bitcast.7) | data formatting | bytes 131072
Async XLA Ops:
  34.5 1.5 %copy-start = (bf16[256,128]{1,0:T(8,128)(2,1)S(1)}, bf16[256,128]{1,0:T(8,128)(2,1)}, u32[]{:S(2)}) copy-start(bf16[256,128]{1,0:T(8,128)(2,1)} %get-tuple-element.5) | copy-start | bytes 196612

commit v4 on v3

--- a/solution.py
+++ b/solution.py
@@ -34,17 +34,16 @@
     owner_ref,
     offset_ref,
     q_ref,
-    k_ref,
     v_ref,
-    vt_ref,
+    near_k,
+    near_v,
+    far_k,
+    far_v,
+    near_dead,
+    far_dead,
     qz_ref,
-    qx_ref,
     own_o,
     own_l,
-    sx_o,
-    sx_l,
-    rx_o,
-    rx_l,
     sz_o,
     sz_l,
     rz_o,
@@ -53,12 +52,20 @@
     local_sem,
     qz_send,
     qz_recv,
-    qx_send,
-    qx_recv,
-    xo_send,
-    xo_recv,
-    xl_send,
-    xl_recv,
+    xk_send,
+    xk_recv,
+    xv_send,
+    xv_recv,
+    xd_send,
+    xd_recv,
+    yk_send,
+    yk_recv,
+    yv_send,
+    yv_recv,
+    ck_send,
+    ck_recv,
+    cv_send,
+    cv_recv,
     zo_send,
     zo_recv,
     zl_send,
@@ -71,8 +78,9 @@
     nh_recv,
 ):
     rows, size = queries_ref.shape
-    store_rows = keys_ref.shape[0]
-    page = store_rows // slots
+    chunk = keys_ref.shape[1]
+    chunks_page = heads_axis // slots
+    chips = heads_axis // 2
     new_tok = new_hbm.shape[0] // 2
     scale = math.log2(math.e) / math.sqrt(size)
     store = lax.axis_index("ctx")
@@ -80,6 +88,8 @@
     z = lax.div(store, 2)
     x = lax.rem(store, 2)
     pair = store + 1 - 2 * x
+    core = lax.rem(head, 2)
+    other_core = head + 1 - 2 * core
 
     def along_z(steps):
         return 2 * lax.rem(z + steps, layers) + x
@@ -94,7 +104,7 @@
         pltpu.make_async_copy(offset_hbm, offset_ref, local_sem.at[6]),
     ]
     load_q = pltpu.make_async_copy(queries_ref, q_ref, local_sem.at[0])
-    load_k = pltpu.make_async_copy(keys_ref, k_ref, local_sem.at[1])
+    load_k = pltpu.make_async_copy(keys_ref, near_k, local_sem.at[1])
     load_v = pltpu.make_async_copy(values_ref, v_ref, local_sem.at[2])
     load_q.start()
     load_new.start()
@@ -122,6 +132,19 @@
     ).astype(jnp.bfloat16)
     load_q.wait()
     qz_ref[0] = q_ref[...].T
+    for part in range(heads_axis):
+        near_v[part, pl.ds(size, 16), :] = jnp.ones((16, chunk), jnp.bfloat16)
+        far_v[part, pl.ds(size, 16), :] = jnp.ones((16, chunk), jnp.bfloat16)
+    for load in small:
+        load.wait()
+    for number in range(slots):
+        live = jnp.int32(0)
+        for place in range(slots):
+            hit = (table_ref[0, place] == number) & (place < count_ref[0])
+            live = jnp.where(hit, jnp.int32(1), live)
+        gap = jnp.where(live == 1, jnp.float32(0.0), jnp.float32(FAR))
+        near_dead[pl.ds(8 * number, 8), :] = jnp.full((8, rows), gap, jnp.float32)
+    load_k.wait()
 
     pl.semaphore_wait(barrier, layers + heads_axis - 1)
 
@@ -150,20 +173,53 @@
             qz_ref.at[0], qz_ref.at[slot], qz_send.at[slot], qz_recv.at[slot], {"ctx": along_z(slot)}
         )
 
-    def pass_q(slot):
-        return remote(
-            qz_ref.at[slot], qx_ref.at[slot], qx_send.at[slot], qx_recv.at[slot], {"ctx": pair}
-        )
-
-    first_pass = remote(
-        qz_ref.at[0], qx_ref.at[0], qx_send.at[0], qx_recv.at[0], {"ctx": pair}
+    keys_over = remote(near_k.at[head], far_k.at[head], xk_send, xk_recv, {"ctx": pair})
+    values_over = remote(
+        near_v.at[head, pl.ds(0, size)],
+        far_v.at[head, pl.ds(0, size)],
+        xv_send,
+        xv_recv,
+        {"ctx": pair},
     )
-
-    def cross(slot):
-        return (
-            remote(sx_o.at[slot], rx_o.at[slot], xo_send.at[slot], xo_recv.at[slot], {"ctx": pair}),
-            remote(sx_l.at[slot], rx_l.at[slot], xl_send.at[slot], xl_recv.at[slot], {"ctx": pair}),
-        )
+    dead_over = remote(near_dead, far_dead, xd_send, xd_recv, {"ctx": pair})
+
+    def far_part(buffer, owner, steps):
+        part = lax.rem(owner + 2 * steps, heads_axis)
+        return buffer.at[part, pl.ds(0, buffer.shape[1] - (16 if buffer is far_v else 0))]
+
+    def to_chip(buffer, send_sem, recv_sem, steps):
+        mine = far_part(buffer, head, 0)
+        device = {"head": along_head(2 * steps)}
+        return remote(mine, mine, send_sem.at[steps], recv_sem.at[chips - steps], device)
+
+    def from_chip(buffer, send_sem, recv_sem, steps):
+        theirs = far_part(buffer, head, steps)
+        device = {"head": along_head(2 * steps)}
+        return remote(theirs, theirs, send_sem.at[steps], recv_sem.at[steps], device)
+
+    def to_core(buffer, send_sem, recv_sem, steps):
+        mine = far_part(buffer, head, steps)
+        device = {"head": other_core}
+        return remote(mine, mine, send_sem.at[steps], recv_sem.at[steps], device)
+
+    def from_core(buffer, send_sem, recv_sem, steps):
+        theirs = far_part(buffer, other_core, steps)
+        device = {"head": other_core}
+        return remote(theirs, theirs, send_sem.at[steps], recv_sem.at[steps], device)
+
+    def spread(over, buffer, chip_sems, core_sems):
+        over.wait_recv()
+        for steps in range(1, chips):
+            to_chip(buffer, *chip_sems, steps).start()
+        to_core(buffer, *core_sems, 0).start()
+
+    def spread_on(buffer, chip_sems, core_sems):
+        for steps in range(1, chips):
+            from_chip(buffer, *chip_sems, steps).wait_recv()
+            to_core(buffer, *core_sems, steps).start()
+
+    key_sems = ((yk_send, yk_recv), (ck_send, ck_recv))
+    value_sems = ((yv_send, yv_recv), (cv_send, cv_recv))
 
     def give_back(steps):
         slot = layers - steps
@@ -210,38 +266,29 @@
             theirs, theirs, nh_send.at[slot], nh_recv.at[slot], {"head": along_head(slot)}
         )
 
-    first_pass.start()
+    keys_over.start()
     for steps in range(1, layers):
         send_q(steps).start()
+    load_v.wait()
+    near_v[head, pl.ds(0, size), :] = v_ref[head].T
+    values_over.start()
+    dead_over.start()
     for steps in range(1, layers):
         new_z(steps).start()
 
-    for load in small:
-        load.wait()
-    dead = []
-    for number in range(slots):
-        live = jnp.int32(0)
-        for place in range(slots):
-            hit = (table_ref[0, place] == number) & (place < count_ref[0])
-            live = jnp.where(hit, jnp.int32(1), live)
-        dead.append(jnp.where(live == 1, jnp.float32(0.0), jnp.float32(FAR)))
-
-    def partial(query_columns):
-        scores, top = [], None
-        for number in range(slots):
-            found = jnp.dot(
-                k_ref[pl.ds(number * page, page), :],
-                query_columns,
-                preferred_element_type=jnp.float32,
-            )
+    def partial(query_columns, keys, values, gaps):
+        scores, top, dead = [], None, []
+        for number in range(heads_axis):
+            found = jnp.dot(keys[number], query_columns, preferred_element_type=jnp.float32)
             scores.append(found)
+            dead.append(gaps[pl.ds(8 * (number // chunks_page), 1), :])
             page_top = jnp.max(found, axis=0, keepdims=True) - dead[number]
             top = page_top if top is None else jnp.maximum(top, page_top)
         summed = None
-        for number in range(slots):
+        for number in range(heads_axis):
             weights = jnp.exp2((scores[number] - (top + dead[number])) * scale)
             product = jnp.dot(
-                vt_ref[:, pl.ds(number * page, page)],
+                values[number],
                 weights.astype(jnp.bfloat16),
                 preferred_element_type=jnp.float32,
             )
@@ -267,50 +314,24 @@
         summed = functools.reduce(jnp.add, [one * mean for one, (mean, _) in zip(share, parts)])
         return summed / whole, top + jnp.log2(whole)
 
-    def join_pair(slot):
-        for copy in cross(slot):
-            copy.wait_recv()
-        return merged(
-            [
-                (own_o[slot], own_l[slot, 0:1, :]),
-                read(rx_o.at[slot], rx_l.at[slot]),
-            ]
-        )
-
-    def send_joined(slot):
-        mean, level = join_pair(slot)
-        write(mean, level, sz_o.at[slot], sz_l.at[slot])
-        for copy in give_back(slot):
-            copy.start()
-
-    def serve_pair(slot):
-        mean, level = partial(qx_ref[slot])
-        write(mean, level, sx_o.at[slot], sx_l.at[slot])
-        for copy in cross(slot):
-            copy.start()
-
-    load_k.wait()
-    load_v.wait()
-    vt_ref[pl.ds(0, size), :] = v_ref[...].T
-    vt_ref[pl.ds(size, 16), :] = jnp.ones((16, store_rows), jnp.bfloat16)
-    mean, level = partial(qz_ref[0])
-    own_o[0] = mean
-    own_l[0, 0:1, :] = level
-    take_q(1).wait_recv()
-    pass_q(1).start()
-
-    def layer_step(slot, carry):
-        mean, level = partial(qz_ref[slot])
+    def near_step(slot):
+        mean, level = partial(qz_ref[slot], near_k, near_v, near_dead)
         own_o[slot] = mean
         own_l[slot, 0:1, :] = level
 
-        @pl.when(slot < layers - 1)
-        def _():
-            take_q(slot + 1).wait_recv()
-            pass_q(slot + 1).start()
-
-        pass_q(slot).wait_recv()
-        serve_pair(slot)
+    def far_step(slot):
+        found = partial(qz_ref[slot], far_k, far_v, far_dead)
+        return merged([(own_o[slot], own_l[slot, 0:1, :]), found])
+
+    for step in range(1, heads_axis):
+        part = along_head(step)
+        near_v[part, pl.ds(0, size), :] = v_ref[part].T
+    near_step(0)
+    spread(keys_over, far_k, *key_sems)
+
+    def near_layer(slot, carry):
+        take_q(slot).wait_recv()
+        near_step(slot)
 
         @pl.when(slot == 1)
         def _():
@@ -318,22 +339,18 @@
                 new_z_taken(other).wait_recv()
             new_x(x).start()
 
-        @pl.when(slot >= 2)
-        def _():
-            send_joined(slot - 1)
-
         @pl.when(slot == 2)
         def _():
-            new_x(1 - x).wait_recv()
-            for steps in range(1, heads_axis):
-                new_h(steps).start()
+            spread(values_over, far_v, *value_sems)
 
         return carry
 
-    lax.fori_loop(1, layers, layer_step, 0)
-    first_pass.wait_recv()
-    serve_pair(0)
-    send_joined(layers - 1)
+    lax.fori_loop(1, layers, near_layer, 0)
+    new_x(1 - x).wait_recv()
+    for steps in range(1, heads_axis):
+        new_h(steps).start()
+    spread_on(far_k, *key_sems)
+    spread_on(far_v, *value_sems)
 
     for slot in range(1, heads_axis):
         new_h_taken(slot).wait_recv()
@@ -362,23 +379,41 @@
     summed = jnp.dot(
         new_values.T, weights.astype(jnp.bfloat16), preferred_element_type=jnp.float32
     )
-    parts = [(summed / totals, top * scale + jnp.log2(totals)), join_pair(0)]
+    parts = [(summed / totals, top * scale + jnp.log2(totals))]
+
+    dead_over.wait_recv()
+    for steps in range(chips):
+        from_core(far_k, ck_send, ck_recv, steps).wait_recv()
+        from_core(far_v, cv_send, cv_recv, steps).wait_recv()
+
+    def far_layer(slot, carry):
+        mean, level = far_step(slot)
+        write(mean, level, sz_o.at[slot], sz_l.at[slot])
+        for copy in give_back(slot):
+            copy.start()
+        return carry
+
+    lax.fori_loop(1, layers, far_layer, 0)
+    parts.append(far_step(0))
     for slot in range(1, layers):
         for copy in get_back(slot):
             copy.wait_recv()
         parts.append(read(rz_o.at[slot], rz_l.at[slot]))
     attended_ref[...] = merged(parts)[0].T.astype(jnp.bfloat16)
 
-    first_pass.wait_send()
-    for slot in range(layers):
-        for copy in cross(slot):
+    for copy in (keys_over, values_over, dead_over):
+        copy.wait_send()
+    for steps in range(chips):
+        if steps:
+            to_chip(far_k, yk_send, yk_recv, steps).wait_send()
+            to_chip(far_v, yv_send, yv_recv, steps).wait_send()
+        to_core(far_k, ck_send, ck_recv, steps).wait_send()
+        to_core(far_v, cv_send, cv_recv, steps).wait_send()
+    for slot in range(1, layers):
+        send_q(slot).wait_send()
+        new_z(slot).wait_send()
+        for copy in give_back(slot):
             copy.wait_send()
-        if slot:
-            send_q(slot).wait_send()
-            pass_q(slot).wait_send()
-            new_z(slot).wait_send()
-            for copy in give_back(slot):
-                copy.wait_send()
     new_x(x).wait_send()
     for steps in range(1, heads_axis):
         new_h(steps).wait_send()
@@ -390,10 +425,10 @@
     tok_dev, head_dev, size = queries.shape
     new_tok = new_kv.shape[0]
     slots = page_table.shape[1]
-    store_rows = cache_keys.shape[0]
     stores = lax.axis_size("ctx")
     heads_axis = lax.axis_size("head")
     layers = stores // 2
+    chunk = cache_keys.shape[0] // heads_axis
     rows = tok_dev * head_dev
     append_rows = 2 * tok_dev
     tokens = new_owner.shape[0]
@@ -419,16 +454,15 @@
             pltpu.VMEM((1, tokens), jnp.int32),
             pltpu.VMEM((1, tokens), jnp.int32),
             pltpu.VMEM((rows, size), bf16),
-            pltpu.VMEM((store_rows, size), bf16),
-            pltpu.VMEM((store_rows, size), bf16),
-            pltpu.VMEM((size + 16, store_rows), bf16),
-            mean_block,
+            pltpu.VMEM((heads_axis, chunk, size), bf16),
+            pltpu.VMEM((heads_axis, chunk, size), bf16),
+            pltpu.VMEM((heads_axis, size + 16, chunk), bf16),
+            pltpu.VMEM((heads_axis, chunk, size), bf16),
+            pltpu.VMEM((heads_axis, size + 16, chunk), bf16),
+            pltpu.VMEM((8 * slots, rows), f32),
+            pltpu.VMEM((8 * slots, rows), f32),
             mean_block,
             pltpu.VMEM((layers, size, rows), f32),
-            level_block,
-            part_block,
-            level_block,
-            part_block,
             level_block,
             part_block,
             level_block,
@@ -437,7 +471,10 @@
             pltpu.VMEM((layers, 2, heads_axis, 2 * new_tok, size), bf16),
             pltpu.SemaphoreType.DMA((7,)),
         ]
-        + [dma] * 14
+        + [dma] * 2
+        + [pltpu.SemaphoreType.DMA] * 6
+        + [pltpu.SemaphoreType.DMA((heads_axis // 2,))] * 8
+        + [dma] * 6
         + [
             pltpu.SemaphoreType.DMA,
             pltpu.SemaphoreType.DMA,
@@ -451,8 +488,8 @@
         page_table,
         page_count,
         queries.reshape(rows, size),
-        cache_keys,
-        cache_values,
+        cache_keys.reshape(heads_axis, chunk, size),
+        cache_values.reshape(heads_axis, chunk, size),
         new_kv.reshape(2 * new_tok, size),
         new_owner.reshape(1, tokens),
         new_offset.reshape(1, tokens),

time: 36.9 us -> 35.6 us (0.965)
  Pallas kernels: 33.2 us -> 32 us
    pallas_call x1, Pallas kernels: 33.2 us -> 32 us  [shards(): pl.pallas_call(functools.partial(attention_kernel, layers, heads_axis, he...]
where the time goes in v4:
time: 35.6 us; the launch traced here: 35.4 us
  Pallas kernels  32 us (90%)
  local copies, waits for them, and re-layouts  2.16 us (6%)
  between operations  1.29 us (4%)
    pallas_call x1, Pallas kernels, shards(): pl.pallas_call(functools.partial(attention_kernel, layers, heads_axis, he...  32 us
    unnamed x4, local copies, waits for them, and re-layouts  2.16 us

profile of v4, /device:TPU:0, one launch (start us, length us, event | category | flops | bytes accessed | tf_op | source)
XLA Modules:
  0.0 35.4 jit_solution(10014273923899504344)
XLA Ops:
  1.3 32.0 %shard_map.95 = (bf16[256,128]{1,0:T(8,128)(2,1)}, bf16[256,128]{1,0:T(8,128)(2,1)}) custom-call(s32[1,4]{1,0:T(1,128)} %table_hbm.1, s32[1]{0:T(128)S(6)} %copy.12.count_ref, bf16[256,128]{1,0:T(8,128)(2,1)} %bitcast.10, bf16[4,512,128]{2,1,0:T(8,128)(2,1)} %bitcast.8, bf16[4,512,128]{2,1,0:T(8,128)(2,1)} %bitcast.9, bf16[32,128]{1,0:T(8,128)(2,1)} %bitcast.13, ...), custom_call_target="tpu_custom_call" | custom-call | tf_op jit(solution)/shard_map/pallas_call | solution.py:443
  33.3 0.0 copy-start
  33.3 1.5 %copy.13 = bf16[64,4,128]{2,1,0:T(4,128)(2,1)} copy(bf16[64,4,128]{2,1,0:T(4,128)(2,1)} %bitcast.12) | data formatting | bytes 131072
  34.8 0.0 copy-done
  34.8 0.6 %copy.14 = bf16[128,2,128]{2,1,0:T(2,128)(2,1)} copy(bf16[128,2,128]{2,1,0:T(2,128)(2,1)S(1)} %bitcast.11) | data formatting | bytes 131072
Async XLA Ops:
  33.3 1.5 %copy-start = (bf16[256,128]{1,0:T(8,128)(2,1)S(1)}, bf16[256,128]{1,0:T(8,128)(2,1)}, u32[]{:S(2)}) copy-start(bf16[256,128]{1,0:T(8,128)(2,1)} %get-tuple-element.5) | copy-start | bytes 196612

commit v5 on v4

--- a/solution.py
+++ b/solution.py
@@ -12,6 +12,7 @@
 FAR = 1e30
 STEPS = 32767.0
 TINY = 1e-30
+PIECES = 4
 
 
 def attention_kernel(
@@ -132,9 +133,11 @@
     ).astype(jnp.bfloat16)
     load_q.wait()
     qz_ref[0] = q_ref[...].T
+    ones = jnp.ones((16, chunk // PIECES), jnp.bfloat16)
     for part in range(heads_axis):
-        near_v[part, pl.ds(size, 16), :] = jnp.ones((16, chunk), jnp.bfloat16)
-        far_v[part, pl.ds(size, 16), :] = jnp.ones((16, chunk), jnp.bfloat16)
+        for piece in range(PIECES):
+            near_v[part, piece, pl.ds(size, 16), :] = ones
+            far_v[part, piece, pl.ds(size, 16), :] = ones
     for load in small:
         load.wait()
     for number in range(slots):
@@ -158,6 +161,11 @@
             device_id_type=MESH,
         )
 
+    def place_values(part):
+        for piece in range(PIECES):
+            rows_in = pl.ds(piece * (chunk // PIECES), chunk // PIECES)
+            near_v[part, piece, pl.ds(0, size), :] = v_ref[part, rows_in, :].T
+
     def send_q(steps):
         slot = layers - steps
         return remote(
@@ -173,53 +181,89 @@
             qz_ref.at[0], qz_ref.at[slot], qz_send.at[slot], qz_recv.at[slot], {"ctx": along_z(slot)}
         )
 
-    keys_over = remote(near_k.at[head], far_k.at[head], xk_send, xk_recv, {"ctx": pair})
-    values_over = remote(
-        near_v.at[head, pl.ds(0, size)],
-        far_v.at[head, pl.ds(0, size)],
-        xv_send,
-        xv_recv,
-        {"ctx": pair},
-    )
     dead_over = remote(near_dead, far_dead, xd_send, xd_recv, {"ctx": pair})
 
-    def far_part(buffer, owner, steps):
-        part = lax.rem(owner + 2 * steps, heads_axis)
-        return buffer.at[part, pl.ds(0, buffer.shape[1] - (16 if buffer is far_v else 0))]
-
-    def to_chip(buffer, send_sem, recv_sem, steps):
-        mine = far_part(buffer, head, 0)
-        device = {"head": along_head(2 * steps)}
-        return remote(mine, mine, send_sem.at[steps], recv_sem.at[chips - steps], device)
-
-    def from_chip(buffer, send_sem, recv_sem, steps):
-        theirs = far_part(buffer, head, steps)
-        device = {"head": along_head(2 * steps)}
-        return remote(theirs, theirs, send_sem.at[steps], recv_sem.at[steps], device)
-
-    def to_core(buffer, send_sem, recv_sem, steps):
-        mine = far_part(buffer, head, steps)
-        device = {"head": other_core}
-        return remote(mine, mine, send_sem.at[steps], recv_sem.at[steps], device)
-
-    def from_core(buffer, send_sem, recv_sem, steps):
-        theirs = far_part(buffer, other_core, steps)
-        device = {"head": other_core}
-        return remote(theirs, theirs, send_sem.at[steps], recv_sem.at[steps], device)
-
-    def spread(over, buffer, chip_sems, core_sems):
-        over.wait_recv()
-        for steps in range(1, chips):
-            to_chip(buffer, *chip_sems, steps).start()
-        to_core(buffer, *core_sems, 0).start()
-
-    def spread_on(buffer, chip_sems, core_sems):
-        for steps in range(1, chips):
-            from_chip(buffer, *chip_sems, steps).wait_recv()
-            to_core(buffer, *core_sems, steps).start()
-
-    key_sems = ((yk_send, yk_recv), (ck_send, ck_recv))
-    value_sems = ((yv_send, yv_recv), (cv_send, cv_recv))
+    def key_piece(buffer, part, piece):
+        return buffer.at[part, pl.ds(piece * (chunk // PIECES), chunk // PIECES)]
+
+    def value_piece(buffer, part, piece):
+        return buffer.at[part, piece, pl.ds(0, size)]
+
+    def chip_part(owner, steps):
+        return lax.rem(owner + 2 * steps, heads_axis)
+
+    class Travel:
+        def __init__(self, near, far, piece_of, sems):
+            self.near, self.far, self.piece_of = near, far, piece_of
+            self.x_send, self.x_recv, self.y_send, self.y_recv, self.c_send, self.c_recv = sems
+
+        def over(self, piece):
+            return remote(
+                self.piece_of(self.near, head, piece),
+                self.piece_of(self.far, head, piece),
+                self.x_send.at[piece],
+                self.x_recv.at[piece],
+                {"ctx": pair},
+            )
+
+        def to_chip(self, piece, steps):
+            mine = self.piece_of(self.far, head, piece)
+            return remote(
+                mine,
+                mine,
+                self.y_send.at[piece, steps],
+                self.y_recv.at[piece, chips - steps],
+                {"head": along_head(2 * steps)},
+            )
+
+        def from_chip(self, piece, steps):
+            theirs = self.piece_of(self.far, chip_part(head, steps), piece)
+            return remote(
+                theirs,
+                theirs,
+                self.y_send.at[piece, steps],
+                self.y_recv.at[piece, steps],
+                {"head": along_head(2 * steps)},
+            )
+
+        def core(self, owner, piece, steps):
+            block = self.piece_of(self.far, chip_part(owner, steps), piece)
+            return remote(
+                block,
+                block,
+                self.c_send.at[piece, steps],
+                self.c_recv.at[piece, steps],
+                {"head": other_core},
+            )
+
+        def spread(self, piece):
+            self.over(piece).wait_recv()
+            for steps in range(1, chips):
+                self.to_chip(piece, steps).start()
+            self.core(head, piece, 0).start()
+
+        def spread_on(self, piece):
+            for steps in range(1, chips):
+                self.from_chip(piece, steps).wait_recv()
+                self.core(head, piece, steps).start()
+
+        def arrived(self):
+            for piece in range(PIECES):
+                for steps in range(chips):
+                    self.core(other_core, piece, steps).wait_recv()
+
+        def sent(self):
+            for piece in range(PIECES):
+                self.over(piece).wait_send()
+                for steps in range(chips):
+                    if steps:
+                        self.to_chip(piece, steps).wait_send()
+                    self.core(head, piece, steps).wait_send()
+
+    key_sems = (xk_send, xk_recv, yk_send, yk_recv, ck_send, ck_recv)
+    value_sems = (xv_send, xv_recv, yv_send, yv_recv, cv_send, cv_recv)
+    keys = Travel(near_k, far_k, key_piece, key_sems)
+    values = Travel(near_v, far_v, value_piece, value_sems)
 
     def give_back(steps):
         slot = layers - steps
@@ -266,12 +310,14 @@
             theirs, theirs, nh_send.at[slot], nh_recv.at[slot], {"head": along_head(slot)}
         )
 
-    keys_over.start()
+    for piece in range(PIECES):
+        keys.over(piece).start()
     for steps in range(1, layers):
         send_q(steps).start()
     load_v.wait()
-    near_v[head, pl.ds(0, size), :] = v_ref[head].T
-    values_over.start()
+    place_values(head)
+    for piece in range(PIECES):
+        values.over(piece).start()
     dead_over.start()
     for steps in range(1, layers):
         new_z(steps).start()
@@ -288,7 +334,7 @@
         for number in range(heads_axis):
             weights = jnp.exp2((scores[number] - (top + dead[number])) * scale)
             product = jnp.dot(
-                values[number],
+                jnp.concatenate([values[number, piece] for piece in range(PIECES)], axis=1),
                 weights.astype(jnp.bfloat16),
                 preferred_element_type=jnp.float32,
             )
@@ -324,10 +370,9 @@
         return merged([(own_o[slot], own_l[slot, 0:1, :]), found])
 
     for step in range(1, heads_axis):
-        part = along_head(step)
-        near_v[part, pl.ds(0, size), :] = v_ref[part].T
+        place_values(along_head(step))
     near_step(0)
-    spread(keys_over, far_k, *key_sems)
+    keys.spread(0)
 
     def near_layer(slot, carry):
         take_q(slot).wait_recv()
@@ -339,9 +384,11 @@
                 new_z_taken(other).wait_recv()
             new_x(x).start()
 
-        @pl.when(slot == 2)
-        def _():
-            spread(values_over, far_v, *value_sems)
+        for piece in range(1, PIECES):
+
+            @pl.when(slot == piece)
+            def _():
+                keys.spread(piece)
 
         return carry
 
@@ -349,8 +396,14 @@
     new_x(1 - x).wait_recv()
     for steps in range(1, heads_axis):
         new_h(steps).start()
-    spread_on(far_k, *key_sems)
-    spread_on(far_v, *value_sems)
+    keys.spread_on(0)
+    for piece in range(PIECES):
+        values.spread(piece)
+        if piece < PIECES - 1:
+            keys.spread_on(piece + 1)
+        else:
+            for later in range(PIECES):
+                values.spread_on(later)
 
     for slot in range(1, heads_axis):
         new_h_taken(slot).wait_recv()
@@ -382,18 +435,18 @@
     parts = [(summed / totals, top * scale + jnp.log2(totals))]
 
     dead_over.wait_recv()
-    for steps in range(chips):
-        from_core(far_k, ck_send, ck_recv, steps).wait_recv()
-        from_core(far_v, cv_send, cv_recv, steps).wait_recv()
-
-    def far_layer(slot, carry):
+    keys.arrived()
+    values.arrived()
+
+    def far_layer(number, carry):
+        slot = 1 + lax.rem(number + layers // 2 - 1, layers - 1)
         mean, level = far_step(slot)
         write(mean, level, sz_o.at[slot], sz_l.at[slot])
         for copy in give_back(slot):
             copy.start()
         return carry
 
-    lax.fori_loop(1, layers, far_layer, 0)
+    lax.fori_loop(0, layers - 1, far_layer, 0)
     parts.append(far_step(0))
     for slot in range(1, layers):
         for copy in get_back(slot):
@@ -401,14 +454,9 @@
         parts.append(read(rz_o.at[slot], rz_l.at[slot]))
     attended_ref[...] = merged(parts)[0].T.astype(jnp.bfloat16)
 
-    for copy in (keys_over, values_over, dead_over):
-        copy.wait_send()
-    for steps in range(chips):
-        if steps:
-            to_chip(far_k, yk_send, yk_recv, steps).wait_send()
-            to_chip(far_v, yv_send, yv_recv, steps).wait_send()
-        to_core(far_k, ck_send, ck_recv, steps).wait_send()
-        to_core(far_v, cv_send, cv_recv, steps).wait_send()
+    dead_over.wait_send()
+    keys.sent()
+    values.sent()
     for slot in range(1, layers):
         send_q(slot).wait_send()
         new_z(slot).wait_send()
@@ -456,9 +504,9 @@
             pltpu.VMEM((rows, size), bf16),
             pltpu.VMEM((heads_axis, chunk, size), bf16),
             pltpu.VMEM((heads_axis, chunk, size), bf16),
-            pltpu.VMEM((heads_axis, size + 16, chunk), bf16),
+            pltpu.VMEM((heads_axis, PIECES, size + 16, chunk // PIECES), bf16),
             pltpu.VMEM((heads_axis, chunk, size), bf16),
-            pltpu.VMEM((heads_axis, size + 16, chunk), bf16),
+            pltpu.VMEM((heads_axis, PIECES, size + 16, chunk // PIECES), bf16),
             pltpu.VMEM((8 * slots, rows), f32),
             pltpu.VMEM((8 * slots, rows), f32),
             mean_block,
@@ -472,8 +520,9 @@
             pltpu.SemaphoreType.DMA((7,)),
         ]
         + [dma] * 2
-        + [pltpu.SemaphoreType.DMA] * 6
-        + [pltpu.SemaphoreType.DMA((heads_axis // 2,))] * 8
+        + [pltpu.SemaphoreType.DMA((PIECES,))] * 4
+        + [pltpu.SemaphoreType.DMA] * 2
+        + [pltpu.SemaphoreType.DMA((PIECES, heads_axis // 2))] * 8
         + [dma] * 6
         + [
             pltpu.SemaphoreType.DMA,

time: 35.6 us -> 39.2 us (1.10)
  Pallas kernels: 32 us -> 35.6 us
    pallas_call x1, Pallas kernels: 32 us -> 35.6 us  [shards(): pl.pallas_call(functools.partial(attention_kernel, layers, heads_axis, he...]
where the time goes in v5:
time: 39.2 us; the launch traced here: 39 us
  Pallas kernels  35.6 us (91%)
  local copies, waits for them, and re-layouts  2.16 us (6%)
  between operations  1.29 us (3%)
    pallas_call x1, Pallas kernels, shards(): pl.pallas_call(functools.partial(attention_kernel, layers, heads_axis, he...  35.6 us
    unnamed x4, local copies, waits for them, and re-layouts  2.16 us

profile of v5, /device:TPU:0, one launch (start us, length us, event | category | flops | bytes accessed | tf_op | source)
XLA Modules:
  0.0 39.0 jit_solution(7341574216648422486)
XLA Ops:
  1.3 35.6 %shard_map.95 = (bf16[256,128]{1,0:T(8,128)(2,1)}, bf16[256,128]{1,0:T(8,128)(2,1)}) custom-call(s32[1,4]{1,0:T(1,128)} %table_hbm.1, s32[1]{0:T(128)S(6)} %copy.12.count_ref, bf16[256,128]{1,0:T(8,128)(2,1)} %bitcast.10, bf16[4,512,128]{2,1,0:T(8,128)(2,1)} %bitcast.8, bf16[4,512,128]{2,1,0:T(8,128)(2,1)} %bitcast.9, bf16[32,128]{1,0:T(8,128)(2,1)} %bitcast.13, ...), custom_call_target="tpu_custom_call" | custom-call | tf_op jit(solution)/shard_map/pallas_call | solution.py:491
  36.9 0.0 copy-start
  36.9 1.5 %copy.13 = bf16[64,4,128]{2,1,0:T(4,128)(2,1)} copy(bf16[64,4,128]{2,1,0:T(4,128)(2,1)} %bitcast.12) | data formatting | bytes 131072
  38.4 0.0 copy-done
  38.4 0.6 %copy.14 = bf16[128,2,128]{2,1,0:T(2,128)(2,1)} copy(bf16[128,2,128]{2,1,0:T(2,128)(2,1)S(1)} %bitcast.11) | data formatting | bytes 131072
Async XLA Ops:
  36.9 1.5 %copy-start = (bf16[256,128]{1,0:T(8,128)(2,1)S(1)}, bf16[256,128]{1,0:T(8,128)(2,1)}, u32[]{:S(2)}) copy-start(bf16[256,128]{1,0:T(8,128)(2,1)} %get-tuple-element.5) | copy-start | bytes 196612

commit v6 on v3

--- a/solution.py
+++ b/solution.py
@@ -296,21 +296,20 @@
     mean, level = partial(qz_ref[0])
     own_o[0] = mean
     own_l[0, 0:1, :] = level
+    first_pass.wait_recv()
+    serve_pair(0)
     take_q(1).wait_recv()
     pass_q(1).start()
 
-    def layer_step(slot, carry):
+    def serve_own(slot):
         mean, level = partial(qz_ref[slot])
         own_o[slot] = mean
         own_l[slot, 0:1, :] = level
 
-        @pl.when(slot < layers - 1)
-        def _():
-            take_q(slot + 1).wait_recv()
-            pass_q(slot + 1).start()
-
-        pass_q(slot).wait_recv()
-        serve_pair(slot)
+    def layer_step(slot, carry):
+        serve_own(slot)
+        take_q(slot + 1).wait_recv()
+        pass_q(slot + 1).start()
 
         @pl.when(slot == 1)
         def _():
@@ -322,18 +321,20 @@
         def _():
             send_joined(slot - 1)
 
-        @pl.when(slot == 2)
-        def _():
-            new_x(1 - x).wait_recv()
-            for steps in range(1, heads_axis):
-                new_h(steps).start()
-
+        pass_q(slot).wait_recv()
+        serve_pair(slot)
         return carry
 
-    lax.fori_loop(1, layers, layer_step, 0)
-    first_pass.wait_recv()
-    serve_pair(0)
-    send_joined(layers - 1)
+    last = layers - 1
+    lax.fori_loop(1, last, layer_step, 0)
+    new_x(1 - x).wait_recv()
+    for steps in range(1, heads_axis):
+        new_h(steps).start()
+    pass_q(last).wait_recv()
+    serve_pair(last)
+    send_joined(last - 1)
+    serve_own(last)
+    send_joined(last)
 
     for slot in range(1, heads_axis):
         new_h_taken(slot).wait_recv()

time: 36.9 us -> 36.3 us (0.984)
  Pallas kernels: 33.2 us -> 32.6 us
    pallas_call x1, Pallas kernels: 33.2 us -> 32.6 us  [shards(): pl.pallas_call(functools.partial(attention_kernel, layers, heads_axis, he...]
where the time goes in v6:
time: 36.3 us; the launch traced here: 36.1 us
  Pallas kernels  32.6 us (90%)
  local copies, waits for them, and re-layouts  2.16 us (6%)
  between operations  1.29 us (4%)
    pallas_call x1, Pallas kernels, shards(): pl.pallas_call(functools.partial(attention_kernel, layers, heads_axis, he...  32.6 us
    unnamed x4, local copies, waits for them, and re-layouts  2.16 us

profile of v6, /device:TPU:0, one launch (start us, length us, event | category | flops | bytes accessed | tf_op | source)
XLA Modules:
  0.0 36.1 jit_solution(4391646087238869510)
XLA Ops:
  1.3 32.6 %shard_map.95 = (bf16[256,128]{1,0:T(8,128)(2,1)}, bf16[256,128]{1,0:T(8,128)(2,1)}) custom-call(s32[1,4]{1,0:T(1,128)} %table_hbm.1, s32[1]{0:T(128)S(6)} %copy.12.count_ref, bf16[256,128]{1,0:T(8,128)(2,1)} %bitcast.6, bf16[2048,128]{1,0:T(8,128)(2,1)} %keys_ref.1, bf16[2048,128]{1,0:T(8,128)(2,1)} %values_ref.1, bf16[32,128]{1,0:T(8,128)(2,1)} %bitcast.9, ...), custom_call_target="tpu_custom_call" | custom-call | tf_op jit(solution)/shard_map/pallas_call | solution.py:409
  33.9 0.0 copy-start
  33.9 1.5 %copy.13 = bf16[64,4,128]{2,1,0:T(4,128)(2,1)} copy(bf16[64,4,128]{2,1,0:T(4,128)(2,1)} %bitcast.8) | data formatting | bytes 131072
  35.4 0.0 copy-done
  35.4 0.6 %copy.14 = bf16[128,2,128]{2,1,0:T(2,128)(2,1)} copy(bf16[128,2,128]{2,1,0:T(2,128)(2,1)S(1)} %bitcast.7) | data formatting | bytes 131072
Async XLA Ops:
  33.9 1.5 %copy-start = (bf16[256,128]{1,0:T(8,128)(2,1)S(1)}, bf16[256,128]{1,0:T(8,128)(2,1)}, u32[]{:S(2)}) copy-start(bf16[256,128]{1,0:T(8,128)(2,1)} %get-tuple-element.5) | copy-start | bytes 196612

commit v7 on v4

--- a/solution.py
+++ b/solution.py
@@ -41,6 +41,8 @@
     far_v,
     near_dead,
     far_dead,
+    score_ref,
+    sum_ref,
     qz_ref,
     own_o,
     own_l,
@@ -277,22 +279,27 @@
         new_z(steps).start()
 
     def partial(query_columns, keys, values, gaps):
-        scores, top, dead = [], None, []
-        for number in range(heads_axis):
+        def gap(number):
+            first = pl.multiple_of(8 * lax.div(number, chunks_page), 8)
+            return gaps[pl.ds(first, 8), :][0:1, :]
+
+        def score(number, top):
             found = jnp.dot(keys[number], query_columns, preferred_element_type=jnp.float32)
-            scores.append(found)
-            dead.append(gaps[pl.ds(8 * (number // chunks_page), 1), :])
-            page_top = jnp.max(found, axis=0, keepdims=True) - dead[number]
-            top = page_top if top is None else jnp.maximum(top, page_top)
-        summed = None
-        for number in range(heads_axis):
-            weights = jnp.exp2((scores[number] - (top + dead[number])) * scale)
-            product = jnp.dot(
-                values[number],
-                weights.astype(jnp.bfloat16),
-                preferred_element_type=jnp.float32,
+            score_ref[number] = found
+            return jnp.maximum(top, jnp.max(found, axis=0, keepdims=True) - gap(number))
+
+        def weigh(number, carry):
+            weights = jnp.exp2((score_ref[number] - (top + gap(number))) * scale)
+            sum_ref[...] += jnp.dot(
+                values[number], weights.astype(jnp.bfloat16), preferred_element_type=jnp.float32
             )
-            summed = product if summed is None else summed + product
+            return carry
+
+        lowest = jnp.full((1, rows), -3.0 * FAR, jnp.float32)
+        top = lax.fori_loop(0, heads_axis, score, lowest)
+        sum_ref[...] = jnp.zeros_like(sum_ref)
+        lax.fori_loop(0, heads_axis, weigh, 0)
+        summed = sum_ref[...]
         totals = summed[size : size + 1, :]
         return summed[:size, :] / totals, top * scale + jnp.log2(totals)
 
@@ -326,12 +333,16 @@
     for step in range(1, heads_axis):
         part = along_head(step)
         near_v[part, pl.ds(0, size), :] = v_ref[part].T
-    near_step(0)
-    spread(keys_over, far_k, *key_sems)
-
     def near_layer(slot, carry):
-        take_q(slot).wait_recv()
+        @pl.when(slot >= 1)
+        def _():
+            take_q(slot).wait_recv()
+
         near_step(slot)
+
+        @pl.when(slot == 0)
+        def _():
+            spread(keys_over, far_k, *key_sems)
 
         @pl.when(slot == 1)
         def _():
@@ -345,7 +356,7 @@
 
         return carry
 
-    lax.fori_loop(1, layers, near_layer, 0)
+    lax.fori_loop(0, layers, near_layer, 0)
     new_x(1 - x).wait_recv()
     for steps in range(1, heads_axis):
         new_h(steps).start()
@@ -386,15 +397,25 @@
         from_core(far_k, ck_send, ck_recv, steps).wait_recv()
         from_core(far_v, cv_send, cv_recv, steps).wait_recv()
 
-    def far_layer(slot, carry):
+    def far_layer(number, carry):
+        slot = lax.rem(number + 1, layers)
         mean, level = far_step(slot)
-        write(mean, level, sz_o.at[slot], sz_l.at[slot])
-        for copy in give_back(slot):
-            copy.start()
+
+        @pl.when(slot >= 1)
+        def _():
+            write(mean, level, sz_o.at[slot], sz_l.at[slot])
+            for copy in give_back(slot):
+                copy.start()
+
+        @pl.when(slot == 0)
+        def _():
+            own_o[0] = mean
+            own_l[0, 0:1, :] = level
+
         return carry
 
-    lax.fori_loop(1, layers, far_layer, 0)
-    parts.append(far_step(0))
+    lax.fori_loop(0, layers, far_layer, 0)
+    parts.append((own_o[0], own_l[0, 0:1, :]))
     for slot in range(1, layers):
         for copy in get_back(slot):
             copy.wait_recv()
@@ -461,6 +482,8 @@
             pltpu.VMEM((heads_axis, size + 16, chunk), bf16),
             pltpu.VMEM((8 * slots, rows), f32),
             pltpu.VMEM((8 * slots, rows), f32),
+            pltpu.VMEM((heads_axis, chunk, rows), f32),
+            pltpu.VMEM((size + 16, rows), f32),
             mean_block,
             pltpu.VMEM((layers, size, rows), f32),
             level_block,

time: 35.6 us -> 39 us (1.096)
  Pallas kernels: 32 us -> 35.3 us
    pallas_call x1, Pallas kernels: 32 us -> 35.3 us  [shards(): pl.pallas_call(functools.partial(attention_kernel, layers, heads_axis, he...]
where the time goes in v7:
time: 39 us; the launch traced here: 38.8 us
  Pallas kernels  35.3 us (91%)
  local copies, waits for them, and re-layouts  2.16 us (6%)
  between operations  1.29 us (3%)
    pallas_call x1, Pallas kernels, shards(): pl.pallas_call(functools.partial(attention_kernel, layers, heads_axis, he...  35.3 us
    unnamed x4, local copies, waits for them, and re-layouts  2.16 us

profile of v7, /device:TPU:0, one launch (start us, length us, event | category | flops | bytes accessed | tf_op | source)
XLA Modules:
  0.0 38.8 jit_solution(13794515558177197060)
XLA Ops:
  1.3 35.3 %shard_map.95 = (bf16[256,128]{1,0:T(8,128)(2,1)}, bf16[256,128]{1,0:T(8,128)(2,1)}) custom-call(s32[1,4]{1,0:T(1,128)} %table_hbm.1, s32[1]{0:T(128)S(6)} %copy.12.count_ref, bf16[256,128]{1,0:T(8,128)(2,1)} %bitcast.10, bf16[4,512,128]{2,1,0:T(8,128)(2,1)} %bitcast.8, bf16[4,512,128]{2,1,0:T(8,128)(2,1)} %bitcast.9, bf16[32,128]{1,0:T(8,128)(2,1)} %bitcast.13, ...), custom_call_target="tpu_custom_call" | custom-call | tf_op jit(solution)/shard_map/pallas_call | solution.py:464
  36.6 0.0 copy-start
  36.6 1.5 %copy.13 = bf16[64,4,128]{2,1,0:T(4,128)(2,1)} copy(bf16[64,4,128]{2,1,0:T(4,128)(2,1)} %bitcast.12) | data formatting | bytes 131072
  38.1 0.0 copy-done
  38.1 0.6 %copy.14 = bf16[128,2,128]{2,1,0:T(2,128)(2,1)} copy(bf16[128,2,128]{2,1,0:T(2,128)(2,1)S(1)} %bitcast.11) | data formatting | bytes 131072
Async XLA Ops:
  36.6 1.5 %copy-start = (bf16[256,128]{1,0:T(8,128)(2,1)S(1)}, bf16[256,128]{1,0:T(8,128)(2,1)}, u32[]{:S(2)}) copy-start(bf16[256,128]{1,0:T(8,128)(2,1)} %get-tuple-element.5) | copy-start | bytes 196612

commit v8 on v4

--- a/solution.py
+++ b/solution.py
@@ -386,14 +386,15 @@
         from_core(far_k, ck_send, ck_recv, steps).wait_recv()
         from_core(far_v, cv_send, cv_recv, steps).wait_recv()
 
-    def far_layer(slot, carry):
+    def far_layer(number, carry):
+        slot = 1 + lax.rem(number + layers // 2 - 1, layers - 1)
         mean, level = far_step(slot)
         write(mean, level, sz_o.at[slot], sz_l.at[slot])
         for copy in give_back(slot):
             copy.start()
         return carry
 
-    lax.fori_loop(1, layers, far_layer, 0)
+    lax.fori_loop(0, layers - 1, far_layer, 0)
     parts.append(far_step(0))
     for slot in range(1, layers):
         for copy in get_back(slot):

time: 35.6 us -> 35.6 us (level)
  no operation moved by 1% of the time
where the time goes in v8:
time: 35.6 us; the launch traced here: 35.4 us
  Pallas kernels  32 us (90%)
  local copies, waits for them, and re-layouts  2.16 us (6%)
  between operations  1.29 us (4%)
    pallas_call x1, Pallas kernels, shards(): pl.pallas_call(functools.partial(attention_kernel, layers, heads_axis, he...  32 us
    unnamed x4, local copies, waits for them, and re-layouts  2.16 us

profile of v8, /device:TPU:0, one launch (start us, length us, event | category | flops | bytes accessed | tf_op | source)
XLA Modules:
  0.0 35.4 jit_solution(2560882031898262818)
XLA Ops:
  1.3 32.0 %shard_map.95 = (bf16[256,128]{1,0:T(8,128)(2,1)}, bf16[256,128]{1,0:T(8,128)(2,1)}) custom-call(s32[1,4]{1,0:T(1,128)} %table_hbm.1, s32[1]{0:T(128)S(6)} %copy.12.count_ref, bf16[256,128]{1,0:T(8,128)(2,1)} %bitcast.10, bf16[4,512,128]{2,1,0:T(8,128)(2,1)} %bitcast.8, bf16[4,512,128]{2,1,0:T(8,128)(2,1)} %bitcast.9, bf16[32,128]{1,0:T(8,128)(2,1)} %bitcast.13, ...), custom_call_target="tpu_custom_call" | custom-call | tf_op jit(solution)/shard_map/pallas_call | solution.py:444
  33.2 0.0 copy-start
  33.3 1.5 %copy.13 = bf16[64,4,128]{2,1,0:T(4,128)(2,1)} copy(bf16[64,4,128]{2,1,0:T(4,128)(2,1)} %bitcast.12) | data formatting | bytes 131072
  34.8 0.0 copy-done
  34.8 0.6 %copy.14 = bf16[128,2,128]{2,1,0:T(2,128)(2,1)} copy(bf16[128,2,128]{2,1,0:T(2,128)(2,1)S(1)} %bitcast.11) | data formatting | bytes 131072
Async XLA Ops:
  33.2 1.5 %copy-start = (bf16[256,128]{1,0:T(8,128)(2,1)S(1)}, bf16[256,128]{1,0:T(8,128)(2,1)}, u32[]{:S(2)}) copy-start(bf16[256,128]{1,0:T(8,128)(2,1)} %get-tuple-element.5) | copy-start | bytes 196612
